TPU v7x, 128 devices: a whole 4x4x4 slice. The times are simulated.
128 devices in a mesh: grp: 2 (over core), dp: 16 (over y, z), sp: 4 (over x).
Axes of the slice: x: 4, y: 4, z: 4, core: 2. Of those that a mesh axis runs over, the one named last changes fastest.
Arguments:
- tokens: bfloat16 [16384, 7168], P(('grp', 'dp', 'sp')), may hold values from -6 to 6
- grad_out: bfloat16 [16384, 7168], P(('grp', 'dp', 'sp')), may hold values from -6 to 6
- expert_ids: int32 [16384, 8], P(('grp', 'dp', 'sp')), may hold values from 0 to 255, all different within a row; in each aligned block of 128 rows (0 to 127, 128 to 255, ...) at most 6 rows name the same one
- gate_codes: int32 [16384, 8], P(('grp', 'dp', 'sp')), may hold values from 1 to 4095
- lengths: int32 [128, 2], P(('grp', 'dp', 'sp')), may hold values from 1 to 64, 96 in all within a row
- w_gate: bfloat16 [8, 7168, 2048], P(('grp', 'sp'), None, 'dp'), may hold values from -0.0625 to 0.0625
- w_up: bfloat16 [8, 7168, 2048], P(('grp', 'sp'), None, 'dp'), may hold values from -0.0625 to 0.0625
- w_down: bfloat16 [8, 2048, 7168], P(('grp', 'sp'), 'dp'), may hold values from -0.125 to 0.125
Outputs:
- grad_tokens: bfloat16 [16384, 7168], P(('grp', 'dp', 'sp'))
- grad_gate_w: bfloat16 [8, 7168, 2048], P(('grp', 'sp'), None, 'dp')
- grad_up_w: bfloat16 [8, 7168, 2048], P(('grp', 'sp'), None, 'dp')
- grad_down_w: bfloat16 [8, 2048, 7168], P(('grp', 'sp'), 'dp')
Inputs may be any that keep to these rules, and one draw needn't show every extreme that they name: `expert_ids`: each row names 8 different experts; no expert is named by more than 6 rows of one device. The 2 lengths of one device sum to 96.
All inputs are finite; a program needn't handle non-finite values.
Results may differ from a plain program's by a relative error of at most 0.019.
Values may be sent and summed in bfloat16 or wider, within the bound.
No kernel may reach another device: no remote copies, remote signals or barrier semaphores. Data moves between devices by JAX's collectives and lax.ppermute only.
A program may use at most 192 MiB of HBM per device.

v0:
```python
import jax
import jax.numpy as jnp
from jax import lax
from jax.sharding import PartitionSpec as P

CAP = 6


GRID_SCALE = 2048.0
HIGHEST = lax.Precision.HIGHEST


def slot_tables(expert_ids, gate_codes, lengths, experts):
    tok_count = expert_ids.shape[0]
    sample_count = lengths.shape[0]
    slot_len = tok_count // sample_count
    position = jnp.arange(tok_count, dtype=jnp.int32)
    sample_of = position // slot_len
    offset = position % slot_len
    samples = jnp.arange(sample_count, dtype=jnp.int32)
    length_here = jnp.sum(
        jnp.where(sample_of[:, None] == samples[None, :], lengths[None, :], 0), axis=1
    )
    is_live = offset < length_here
    expert_hit = expert_ids[:, :, None] == jnp.arange(experts, dtype=jnp.int32)[None, None, :]
    member = jnp.logical_and(jnp.any(expert_hit, axis=1), is_live[:, None]).astype(jnp.int32)
    gate_value = (
        jnp.sum(jnp.where(expert_hit, gate_codes[:, :, None], 0), axis=1).astype(jnp.float32)
        / GRID_SCALE
    )
    slot_rank = jnp.cumsum(member, axis=0, dtype=jnp.int32) - member
    slots = jnp.arange(CAP, dtype=jnp.int32)
    chosen = jnp.logical_and(slot_rank[None, :, :] == slots[:, None, None], member[None, :, :] > 0)
    select = jnp.transpose(chosen, (2, 0, 1)).astype(jnp.float32)
    slot_gate = jnp.einsum("ect,te->ec", select, gate_value, precision=HIGHEST)
    return (select, slot_gate)


def expert_pass(rows, grads, gate_w, up_w, down_w):
    gate_pre = jnp.dot(rows, gate_w, preferred_element_type=jnp.float32)
    up_pre = jnp.dot(rows, up_w, preferred_element_type=jnp.float32)
    logistic = jax.nn.sigmoid(gate_pre)
    hidden = (gate_pre * logistic * up_pre).astype(jnp.bfloat16)
    hidden_grad = lax.dot_general(
        grads, down_w, (((1,), (1,)), ((), ())), preferred_element_type=jnp.float32
    )
    up_grad = (hidden_grad * gate_pre * logistic).astype(jnp.bfloat16)
    gate_grad = (hidden_grad * up_pre * logistic * (1.0 + gate_pre * (1.0 - logistic))).astype(
        jnp.bfloat16
    )
    contract_rows = (((0,), (0,)), ((), ()))
    down_w_grad = lax.dot_general(
        hidden, grads, contract_rows, preferred_element_type=jnp.float32
    ).astype(jnp.bfloat16)
    gate_w_grad = lax.dot_general(
        rows, gate_grad, contract_rows, preferred_element_type=jnp.float32
    ).astype(jnp.bfloat16)
    up_w_grad = lax.dot_general(
        rows, up_grad, contract_rows, preferred_element_type=jnp.float32
    ).astype(jnp.bfloat16)
    return (gate_grad, up_grad, gate_w_grad, up_w_grad, down_w_grad)


def hidden_terms(gate_piece, up_piece, gate_w, up_w):
    contract_hidden = (((1,), (1,)), ((), ()))
    partial_term = lax.dot_general(
        gate_piece, gate_w, contract_hidden, preferred_element_type=jnp.float32
    )
    return partial_term + lax.dot_general(
        up_piece, up_w, contract_hidden, preferred_element_type=jnp.float32
    )


def body(tokens, grad_out, expert_ids, gate_codes, lengths, w_gate, w_up, w_down):
    grp_size = lax.axis_size("grp")
    seq_size = lax.axis_size("sp")
    experts = grp_size * seq_size
    width = tokens.shape[1]
    select_float, slot_gate = slot_tables(expert_ids, gate_codes, lengths[0], experts)
    select = select_float.astype(jnp.bfloat16)
    sent_tokens = jnp.einsum(
        "ect,td->ecd", select, tokens, preferred_element_type=jnp.float32
    ).astype(jnp.bfloat16)
    picked = jnp.einsum("ect,td->ecd", select, grad_out, preferred_element_type=jnp.float32)
    sent_grads = (slot_gate[:, :, None] * picked).astype(jnp.bfloat16)
    gate_w = w_gate[0]
    up_w = w_up[0]
    down_w = w_down[0]
    recv_tokens, recv_grads = (
        lax.all_to_all(sent_tokens, ("grp", "sp"), split_axis=0, concat_axis=0, tiled=True),
        lax.all_to_all(sent_grads, ("grp", "sp"), split_axis=0, concat_axis=0, tiled=True),
    )
    all_tokens, all_grads = (
        lax.all_gather(recv_tokens, "dp", axis=0, tiled=True),
        lax.all_gather(recv_grads, "dp", axis=0, tiled=True),
    )
    rows = all_tokens.reshape(-1, width)
    grads = all_grads.reshape(-1, width)
    gate_grad, up_grad, gate_w_grad, up_w_grad, down_w_grad = expert_pass(
        rows, grads, gate_w, up_w, down_w
    )
    summed = lax.psum_scatter(
        hidden_terms(gate_grad, up_grad, gate_w, up_w).astype(jnp.bfloat16),
        "dp",
        scatter_dimension=0,
        tiled=True,
    )
    slot_grad = summed.reshape(experts, CAP, width)
    returned = lax.all_to_all(slot_grad, ("grp", "sp"), split_axis=0, concat_axis=0, tiled=True)
    grad_tokens = jnp.einsum(
        "ect,ecd->td", select, returned, preferred_element_type=jnp.float32
    ).astype(jnp.bfloat16)
    return (grad_tokens, gate_w_grad[None], up_w_grad[None], down_w_grad[None])


def solution(mesh):
    return jax.shard_map(
        body,
        mesh=mesh,
        in_specs=(
            P(("grp", "dp", "sp"), None),
            P(("grp", "dp", "sp"), None),
            P(("grp", "dp", "sp"), None),
            P(("grp", "dp", "sp"), None),
            P(("grp", "dp", "sp"), None),
            P(("grp", "sp"), None, "dp"),
            P(("grp", "sp"), None, "dp"),
            P(("grp", "sp"), "dp", None),
        ),
        out_specs=(
            P(("grp", "dp", "sp"), None),
            P(("grp", "sp"), None, "dp"),
            P(("grp", "sp"), None, "dp"),
            P(("grp", "sp"), "dp", None),
        ),
        check_vma=False,
    )
```

profile of v0, /device:TPU:1, one launch (start us, length us, event | category | flops | bytes accessed | tf_op | source)
XLA Modules:
  0.0 380.4 jit_solution(6323116944534578789)
XLA Ops:
  7.2 0.0 copy-start
  7.2 0.0 all-gather.5.cloned.1.call-start
  7.2 0.9 fusion.22
  8.1 0.7 fusion.18
  8.8 0.1 copy.42
  8.9 0.1 compare_bitcast_fusion
  9.0 0.1 copy.44
  9.1 0.2 reduce_window_sum.11
  9.3 0.1 subtract_bitcast_fusion
  9.4 1.9 convolution_convert_fusion.3
  11.3 0.4 copy.48
  11.7 0.0 copy-start.4
  11.7 0.0 copy-start.5
  11.8 19.2 %all_to_all.15 = bf16[8,6,7168]{2,1,0:T(8,128)(2,1)S(1)} all-to-all(bf16[8,6,7168]{2,1,0:T(8,128)(2,1)S(1)} %copy.48), channel_id=1, replica_groups=mesh['grp'=2,'dp'=16,'sp'=4] {'grp','sp'}, dimensions={0} | all-to-all | bytes 1376256 | tf_op jit(solution)/shard_map/all_to_all | solution.py:90
  30.9 1.2 copy.49
  32.2 0.0 all-gather.5.cloned.1.call-update
  32.2 0.0 all-gather.3.cloned.1.call-start
  32.3 0.0 copy-done.4
  32.3 0.0 copy-done.5
  32.3 0.2 fusion.19
  32.5 0.1 copy.54
  32.6 1.9 fusion.4
  34.4 0.4 copy.45
  34.8 17.2 %all_to_all.16 = bf16[8,6,7168]{2,1,0:T(8,128)(2,1)S(1)} all-to-all(bf16[8,6,7168]{2,1,0:T(8,128)(2,1)S(1)} %copy.45), channel_id=1, replica_groups=mesh['grp'=2,'dp'=16,'sp'=4] {'grp','sp'}, dimensions={0} | all-to-all | bytes 1376256 | tf_op jit(solution)/shard_map/all_to_all | solution.py:91
  52.0 1.2 copy.46
  53.3 0.0 all-gather.3.cloned.1.call-update
  53.3 0.2 reduce-scatter.2.cloned.1.call-start
  53.5 62.6 %all-gather.5.cloned.1.call-done = bf16[128,6,7168]{2,0,1:T(8,128)(2,1)} async-done(((bf16[8,6,7168]{2,0,1:T(8,128)(2,1)}), bf16[128,6,7168]{2,0,1:T(8,128)(2,1)}) %all-gather.5.cloned.1.call-update) | async-done | bytes 11010064 | tf_op jit(solution)/shard_map/all_gather | solution.py:94
  116.1 12.9 %copy.50 = bf16[128,6,7168]{2,1,0:T(8,128)(2,1)} copy(bf16[128,6,7168]{2,0,1:T(8,128)(2,1)} %all-gather.5.cloned.1.call-done) | data formatting | bytes 22020096 | tf_op jit(solution)/shard_map/all_gather | solution.py:94
  129.0 16.5 %reshape.97 = bf16[768,7168]{1,0:T(8,128)(2,1)} reshape(bf16[128,6,7168]{2,1,0:T(8,128)(2,1)} %copy.50) | data formatting | bytes 22020096 | tf_op jit(solution)/shard_map/reshape | solution.py:97
  145.5 0.0 copy-done
  145.5 0.0 copy-start.2
  145.5 0.0 copy-start.3
  145.5 7.1 %fusion.7 = f32[768,128]{1,0:T(8,128)S(1)} fusion(bf16[768,7168]{1,0:T(8,128)(2,1)} %reshape.97, bf16[1,7168,128]{2,1,0:T(8,128)(2,1)S(1)} %copy-done), kind=kOutput, calls=%fused_computation.14 | convolution fusion | flops 1409286144 | bytes 13238272 | tf_op jit(solution)/shard_map/dot_general | solution.py:40
  152.6 0.2 copy-done.2
  152.8 0.5 copy-done.3
  153.3 3.0 fusion.10
  156.3 45.0 %all-gather.3.cloned.1.call-done = bf16[128,6,7168]{2,0,1:T(8,128)(2,1)} async-done(((bf16[8,6,7168]{2,0,1:T(8,128)(2,1)}), bf16[128,6,7168]{2,0,1:T(8,128)(2,1)}) %all-gather.3.cloned.1.call-update) | async-done | bytes 11010064 | tf_op jit(solution)/shard_map/all_gather | solution.py:95
  201.3 12.9 %copy.47 = bf16[128,6,7168]{2,1,0:T(8,128)(2,1)} copy(bf16[128,6,7168]{2,0,1:T(8,128)(2,1)} %all-gather.3.cloned.1.call-done) | data formatting | bytes 22020096 | tf_op jit(solution)/shard_map/all_gather | solution.py:95
  214.2 16.4 %reshape.96 = bf16[768,7168]{1,0:T(8,128)(2,1)} reshape(bf16[128,6,7168]{2,1,0:T(8,128)(2,1)} %copy.47) | data formatting | bytes 22020096 | tf_op jit(solution)/shard_map/reshape | solution.py:98
  230.7 7.6 %multiply_convert_fusion.1 = (bf16[768,128]{1,0:T(8,128)(2,1)S(1)}, bf16[768,128]{1,0:T(8,128)(2,1)S(1)}) fusion(f32[768,128]{1,0:T(8,128)S(1)} %fusion.7, f32[768,128]{1,0:T(8,128)S(1)} %fusion.10, bf16[768,7168]{1,0:T(8,128)(2,1)} %reshape.96, bf16[1,128,7168]{2,1,0:T(8,128)(2,1)} %param.15), kind=kOutput, calls=%fused_computation.25 | convolution fusion | flops 1410564096 | bytes 14024704 | tf_op jit(solution)/shard_map/dot_general | solution.py:44
  238.3 9.2 %fusion.5 = f32[768,7168]{1,0:T(8,128)} fusion(bf16[768,128]{1,0:T(8,128)(2,1)S(1)} %get-tuple-element.5, bf16[1,7168,128]{2,1,0:T(8,128)(2,1)S(1)} %copy-done), kind=kOutput, calls=%fused_computation.12 | convolution fusion | flops 1409286144 | bytes 24051712 | tf_op jit(solution)/shard_map/dot_general | solution.py:66
  247.5 13.2 %add_convert_fusion = bf16[768,7168]{1,0:T(8,128)(2,1)} fusion(f32[768,7168]{1,0:T(8,128)} %fusion.5, bf16[768,128]{1,0:T(8,128)(2,1)S(1)} %get-tuple-element.4, bf16[1,7168,128]{2,1,0:T(8,128)(2,1)} %param.14), kind=kOutput, calls=%fused_computation | convolution fusion | flops 1420296192 | bytes 35061760 | tf_op jit(solution)/shard_map/dot_general | solution.py:69
  260.6 0.0 reduce-scatter.2.cloned.1.call-update
  260.7 8.5 %fusion.3 = bf16[1,7168,128]{2,1,0:T(8,128)(2,1)} fusion(bf16[768,7168]{1,0:T(8,128)(2,1)} %reshape.97, bf16[768,128]{1,0:T(8,128)(2,1)S(1)} %get-tuple-element.4), kind=kOutput, calls=%fused_computation.8 | convolution fusion | flops 1410203648 | bytes 13041664 | tf_op jit(solution)/shard_map/dot_general | solution.py:58
  269.1 8.9 %fusion.2 = bf16[1,7168,128]{2,1,0:T(8,128)(2,1)} fusion(bf16[768,7168]{1,0:T(8,128)(2,1)} %reshape.97, bf16[768,128]{1,0:T(8,128)(2,1)S(1)} %get-tuple-element.5), kind=kOutput, calls=%fused_computation.7 | convolution fusion | flops 1410203648 | bytes 13041664 | tf_op jit(solution)/shard_map/dot_general | solution.py:55
  278.0 72.6 %reduce-scatter.2.cloned.1.call-done = bf16[48,7168]{1,0:T(8,128)(2,1)} async-done(((bf16[768,7168]{1,0:T(8,128)(2,1)}), bf16[48,7168]{1,0:T(8,128)(2,1)}) %reduce-scatter.2.cloned.1.call-update) | async-done | bytes 688144 | tf_op jit(solution)/shard_map/reduce_scatter | solution.py:102
  350.7 2.3 reshape.98
  352.9 5.4 %all-to-all-start.2 = ((bf16[8,6,7168]{2,1,0:T(8,128)(2,1)}), bf16[8,6,7168]{2,1,0:T(8,128)(2,1)S(1)}, u32[]{:S(2)}, u32[]{:S(2)}) async-start(bf16[8,6,7168]{2,1,0:T(8,128)(2,1)} %reshape.98), calls=%async_computation.3 | async-start | bytes 1835008 | tf_op jit(solution)/shard_map/all_to_all | solution.py:109
  358.3 0.0 copy-start.1
  358.4 7.2 %fusion.1 = bf16[1,128,7168]{2,1,0:T(8,128)(2,1)} fusion(bf16[768,7168]{1,0:T(8,128)(2,1)} %reshape.96, f32[768,128]{1,0:T(8,128)S(1)} %fusion.10, f32[768,128]{1,0:T(8,128)S(1)} %fusion.7), kind=kOutput, calls=%fused_computation.6 | convolution fusion | flops 1410793472 | bytes 13631488 | tf_op jit(solution)/shard_map/dot_general | solution.py:52
  365.6 6.4 %all-to-all-done.2 = bf16[8,6,7168]{2,1,0:T(8,128)(2,1)S(1)} async-done(((bf16[8,6,7168]{2,1,0:T(8,128)(2,1)}), bf16[8,6,7168]{2,1,0:T(8,128)(2,1)S(1)}, u32[]{:S(2)}, u32[]{:S(2)}) %all-to-all-start.2) | async-done | bytes 688160 | tf_op jit(solution)/shard_map/all_to_all | solution.py:109
  371.9 1.9 fusion
  373.9 0.0 copy-done.1
  (6 shorter events, 0.1 us)
Async XLA Ops:
  7.2 138.3 %copy-start = (bf16[1,7168,128]{2,1,0:T(8,128)(2,1)S(1)}, bf16[1,7168,128]{2,1,0:T(8,128)(2,1)}, u32[]{:S(2)}) copy-start(bf16[1,7168,128]{2,1,0:T(8,128)(2,1)} %param.13) | copy-start | bytes 5505028
  7.2 108.9 %all-gather.5.cloned.1.call-start = ((), (), s32[]{:S(2)}) async-start(), calls=%async_computation.5 | async-start | bytes 11698176 | tf_op jit(solution)/shard_map/all_gather | solution.py:94
  11.7 20.5 %copy-start.4 = (s32[128,8]{0,1:T(8,128)S(1)}, s32[128,8]{0,1:T(8,128)}, u32[]{:S(2)}) copy-start(s32[128,8]{0,1:T(8,128)} %param.10) | copy-start | bytes 12292
  11.7 20.5 %copy-start.5 = (s32[128,8]{0,1:T(8,128)S(1)}, s32[128,8]{0,1:T(8,128)}, u32[]{:S(2)}) copy-start(s32[128,8]{0,1:T(8,128)} %param.11) | copy-start | bytes 12292
  32.2 169.1 %all-gather.3.cloned.1.call-start = ((), (), s32[]{:S(2)}) async-start(), calls=%async_computation.4 | async-start | bytes 11698176 | tf_op jit(solution)/shard_map/all_gather | solution.py:95
  53.3 297.4 %reduce-scatter.2.cloned.1.call-start = ((), (), s32[]{:S(2)}) async-start(), calls=%async_computation.6 | async-start | bytes 11698176 | tf_op jit(solution)/shard_map/reduce_scatter | solution.py:102
  145.5 7.3 %copy-start.2 = (bf16[768,7168]{1,0:T(8,128)(2,1)S(1)}, bf16[768,7168]{1,0:T(8,128)(2,1)}, u32[]{:S(2)}) copy-start(bf16[768,7168]{1,0:T(8,128)(2,1)} %reshape.97) | copy-start | bytes 33030148
  145.5 7.8 %copy-start.3 = (bf16[1,7168,128]{2,1,0:T(8,128)(2,1)S(1)}, bf16[1,7168,128]{2,1,0:T(8,128)(2,1)}, u32[]{:S(2)}) copy-start(bf16[1,7168,128]{2,1,0:T(8,128)(2,1)} %param.14) | copy-start | bytes 5505028
  352.9 19.0 %all-to-all-start.2 = ((bf16[8,6,7168]{2,1,0:T(8,128)(2,1)}), bf16[8,6,7168]{2,1,0:T(8,128)(2,1)S(1)}, u32[]{:S(2)}, u32[]{:S(2)}) async-start(bf16[8,6,7168]{2,1,0:T(8,128)(2,1)} %reshape.98), calls=%async_computation.3 | async-start | bytes 1835008 | tf_op jit(solution)/shard_map/all_to_all | solution.py:109
  358.3 15.5 %copy-start.1 = (bf16[1,7168,128]{2,1,0:T(8,128)(2,1)S(1)}, bf16[1,7168,128]{2,1,0:T(8,128)(2,1)}, u32[]{:S(2)}) copy-start(bf16[1,7168,128]{2,1,0:T(8,128)(2,1)} %param.13) | copy-start | bytes 5505028
Sparse Core Ops, SparseCore 0:
  32.3 83.7 all-gather.4
  118.8 82.4 all-gather.2
  260.8 89.8 reduce-scatter.1
where the time goes:
time: 382 us; the launch traced here: 380 us
  waiting for transfers between devices  187 us (49%)
  matrix products  70.5 us (18%)
  local copies, waits for them, and re-layouts  65.4 us (17%)
  blocking collectives  36.4 us (10%)
  between operations  13.9 us (4%)
  starting transfers between devices  5.7 us (1%)
    reduce_scatter x1, waiting for transfers between devices, body(): lax.psum_scatter(hidden_terms(gate_grad, up_grad, gate_w, up_w).astype(jn...  72.6 us
    all_gather x1, waiting for transfers between devices, body(): lax.all_gather(recv_tokens, 'dp', axis=0, tiled=True)  62.6 us
    all_gather x1, waiting for transfers between devices, body(): lax.all_gather(recv_grads, 'dp', axis=0, tiled=True)  45 us
    all_to_all x1, blocking collectives, body(): lax.all_to_all(sent_tokens, ('grp', 'sp'), split_axis=0, concat_axis=0, t...  19.2 us
    all_to_all x1, blocking collectives, body(): lax.all_to_all(sent_grads, ('grp', 'sp'), split_axis=0, concat_axis=0, ti...  17.2 us
    reshape x1, local copies, waits for them, and re-layouts, body(): rows = all_tokens.reshape(-1, width)  16.5 us
    reshape x1, local copies, waits for them, and re-layouts, body(): grads = all_grads.reshape(-1, width)  16.4 us
    dot_general x1, matrix products, hidden_terms(): lax.dot_general(up_piece, up_w, contract_hidden, preferred_element_type=j...  13.2 us
  transfers between devices with their start and end apart: 4, of which 4 were waited for; matrix products, arithmetic and copies ran while one was open for 18% of the time, Pallas kernels for 0%

commit v1 on v0

v1 whole, which is shorter than its diff:
```python
import functools

import jax
import jax.numpy as jnp
from jax import lax
from jax.experimental import pallas as pl
from jax.experimental.pallas import tpu as pltpu
from jax.sharding import PartitionSpec as P

CAP = 6
CHUNK = 2
CHUNKS = CAP // CHUNK
PARTS = 4
GRID_SCALE = 2048.0
BF16 = jnp.bfloat16
F32 = jnp.float32
VMEM_LIMIT = 48 * 1024 * 1024


def dot(a, b, contract):
    return lax.dot_general(a, b, (contract, ((), ())), preferred_element_type=F32)


def select_kernel(
    lengths_ref, ids_ref, codes_ref, tok0_ref, tok1_ref, grad0_ref, grad1_ref,
    out0_ref, out1_ref, out2_ref, table_ref, scale_ref,
):
    experts, tok_count = ids_ref.shape[0], ids_ref.shape[1]
    row_count = experts * CHUNK * PARTS

    @pl.when(pl.program_id(0) == 0)
    def _():
        ids = ids_ref[...]
        codes = codes_ref[...]
        slot_len = tok_count // 2
        position = lax.broadcasted_iota(jnp.int32, (1, tok_count), 1)
        bound = jnp.where(
            position < slot_len, lengths_ref[0, 0], lengths_ref[0, 1] + slot_len
        )
        live = position < bound
        expert = lax.broadcasted_iota(jnp.int32, (experts, tok_count), 0)
        member = jnp.zeros((experts, tok_count), F32)
        gate = jnp.zeros((experts, tok_count), F32)
        for e in range(experts):
            hit = ids == e
            found = jnp.sum(hit.astype(F32), axis=0, keepdims=True)
            code = jnp.sum(jnp.where(hit, codes, 0).astype(F32), axis=0, keepdims=True)
            member = jnp.where(
                jnp.logical_and(expert == e, jnp.logical_and(live, found > 0.0)),
                1.0,
                member,
            )
            gate = jnp.where(expert == e, code / GRID_SCALE, gate)
        earlier = lax.broadcasted_iota(jnp.int32, (tok_count, tok_count), 0)
        later = lax.broadcasted_iota(jnp.int32, (tok_count, tok_count), 1)
        before = (earlier < later).astype(BF16)
        rank = dot(member.astype(BF16), before, ((1,), (0,)))
        slot_of = jnp.where(member > 0.0, rank, -1.0)

        def spread(x):
            return jnp.broadcast_to(
                x[:, None, :], (experts, row_count // experts, tok_count)
            ).reshape(row_count, tok_count)

        slot_rows = spread(slot_of)
        gate_rows = spread(gate)
        row = lax.broadcasted_iota(jnp.int32, (row_count, tok_count), 0)
        in_chunk = ((row // PARTS) % CHUNK).astype(F32)
        is_grad = ((row // 2) % 2)[:, :1] == 1
        for c in range(CHUNKS):
            chosen = slot_rows == in_chunk + float(c * CHUNK)
            table_ref[c] = chosen.astype(BF16)
            weight = jnp.sum(jnp.where(chosen, gate_rows, 0.0), axis=1, keepdims=True)
            scale_ref[c] = jnp.broadcast_to(
                jnp.where(is_grad, weight, 1.0), scale_ref.shape[1:]
            )

    row = lax.broadcasted_iota(jnp.int32, (row_count, tok_count), 0)
    pieces = (tok0_ref, tok1_ref, grad0_ref, grad1_ref)
    for c, out_ref in enumerate((out0_ref, out1_ref, out2_ref)):
        table = table_ref[c]
        total = None
        for part in range(PARTS):
            mine = jnp.where(row % PARTS == part, table, jnp.zeros_like(table))
            term = dot(mine, pieces[part][...], ((1,), (0,)))
            total = term if total is None else total + term
        out_ref[...] = (scale_ref[c][:, :1] * total).astype(BF16)


def select_rows(tokens, grad_out, expert_ids, gate_codes, lengths, experts):
    tok_count, width = tokens.shape
    half = width // 2
    tile = 512
    steps = half // tile
    row_count = experts * CHUNK * PARTS
    first = pl.BlockSpec((tok_count, tile), lambda j: (0, j))
    second = pl.BlockSpec((tok_count, tile), lambda j: (0, j + steps))
    whole = pl.BlockSpec((experts, tok_count), lambda j: (0, 0))
    block = pl.BlockSpec((row_count, tile), lambda j: (0, j))
    return pl.pallas_call(
        select_kernel,
        grid=(steps,),
        in_specs=[
            pl.BlockSpec(memory_space=pltpu.SMEM), whole, whole, first, second, first, second,
        ],
        out_specs=[block] * CHUNKS
        + [pl.BlockSpec((CHUNKS, row_count, tok_count), lambda j: (0, 0, 0))],
        out_shape=[jax.ShapeDtypeStruct((row_count, half), BF16)] * CHUNKS
        + [jax.ShapeDtypeStruct((CHUNKS, row_count, tok_count), BF16)],
        scratch_shapes=[pltpu.VMEM((CHUNKS, row_count, 128), F32)],
        compiler_params=pltpu.CompilerParams(vmem_limit_bytes=VMEM_LIMIT),
        name="select_rows",
    )(lengths, expert_ids.T, gate_codes.T, tokens, tokens, grad_out, grad_out)


def unfold_kernel(x_ref, out_ref):
    rows, folded = out_ref.shape[0], x_ref.shape[0]
    to = lax.broadcasted_iota(jnp.int32, (rows, folded), 0)
    src = lax.broadcasted_iota(jnp.int32, (rows, folded), 1)
    pick = (src == to * PARTS + pl.program_id(0)).astype(BF16)
    out_ref[...] = dot(pick, x_ref[...], ((1,), (0,))).astype(BF16)


def unfold(x):
    folded, width = x.shape
    rows = folded // PARTS
    return pl.pallas_call(
        unfold_kernel,
        grid=(PARTS,),
        in_specs=[pl.BlockSpec((folded, width), lambda p: (0, 0))],
        out_specs=pl.BlockSpec((rows, width), lambda p: (0, p)),
        out_shape=jax.ShapeDtypeStruct((rows, width * PARTS), BF16),
        compiler_params=pltpu.CompilerParams(vmem_limit_bytes=VMEM_LIMIT),
        name="unfold",
    )(x)


def fold_kernel(x_ref, out_ref):
    rows, folded = x_ref.shape[0], out_ref.shape[0]
    width = out_ref.shape[1]
    to = lax.broadcasted_iota(jnp.int32, (folded, rows), 0)
    src = lax.broadcasted_iota(jnp.int32, (folded, rows), 1)
    total = None
    for part in range(PARTS):
        place = (to == src * PARTS + part).astype(BF16)
        term = dot(place, x_ref[:, part * width : (part + 1) * width], ((1,), (0,)))
        total = term if total is None else total + term
    out_ref[...] = total.astype(BF16)


def fold(x):
    rows, width = x.shape
    return pl.pallas_call(
        fold_kernel,
        out_shape=jax.ShapeDtypeStruct((rows * PARTS, width // PARTS), BF16),
        compiler_params=pltpu.CompilerParams(vmem_limit_bytes=VMEM_LIMIT),
        name="fold",
    )(x)


def chunk_kernel(rows_ref, grads_ref, gate_w_ref, up_w_ref, down_w_ref,
                 hidden_ref, both_ref, term_ref, gate_acc, up_acc, hid_acc):
    step = pl.program_id(0)
    tiles = pl.num_programs(0) // 2
    tile = rows_ref.shape[1]

    @pl.when(step == 0)
    def _():
        gate_acc[...] = jnp.zeros_like(gate_acc)
        up_acc[...] = jnp.zeros_like(up_acc)
        hid_acc[...] = jnp.zeros_like(hid_acc)

    @pl.when(step < tiles)
    def _():
        span = pl.ds(pl.multiple_of(step * tile, tile), tile)
        rows = rows_ref[...]
        gate_acc[...] += dot(rows, gate_w_ref[span, :], ((1,), (0,)))
        up_acc[...] += dot(rows, up_w_ref[span, :], ((1,), (0,)))
        hid_acc[...] += dot(grads_ref[...], down_w_ref[...], ((1,), (1,)))

    @pl.when(step == tiles - 1)
    def _():
        gate_pre, up_pre, hidden_grad = gate_acc[...], up_acc[...], hid_acc[...]
        logistic = 1.0 / (1.0 + jnp.exp(-gate_pre))
        hidden_ref[...] = (gate_pre * logistic * up_pre).astype(BF16)
        units = gate_pre.shape[1]
        both_ref[:, :units] = (
            hidden_grad * up_pre * logistic * (1.0 + gate_pre * (1.0 - logistic))
        ).astype(BF16)
        both_ref[:, units:] = (hidden_grad * gate_pre * logistic).astype(BF16)

    @pl.when(step >= tiles)
    def _():
        span = pl.ds(pl.multiple_of((step - tiles) * tile, tile), tile)
        units = gate_acc.shape[1]
        term = dot(both_ref[:, :units], gate_w_ref[span, :], ((1,), (1,)))
        term += dot(both_ref[:, units:], up_w_ref[span, :], ((1,), (1,)))
        term_ref[...] = term.astype(BF16)


def chunk_pass(gathered, gate_w, up_w, down_w):
    row_count = gathered.shape[0]
    width, units = gate_w.shape
    tile = 1024
    tiles = width // tile
    last = tiles - 1
    return pl.pallas_call(
        chunk_kernel,
        grid=(2 * tiles,),
        in_specs=[
            pl.BlockSpec((row_count, tile), lambda j: (0, jnp.minimum(j, last))),
            pl.BlockSpec((row_count, tile), lambda j: (0, jnp.minimum(j, last) + tiles)),
            pl.BlockSpec((width, units), lambda j: (0, 0)),
            pl.BlockSpec((width, units), lambda j: (0, 0)),
            pl.BlockSpec((units, tile), lambda j: (0, jnp.minimum(j, last))),
        ],
        out_specs=[
            pl.BlockSpec((row_count, units), lambda j: (0, 0)),
            pl.BlockSpec((row_count, 2 * units), lambda j: (0, 0)),
            pl.BlockSpec((row_count, tile), lambda j: (0, jnp.maximum(j - tiles, 0))),
        ],
        out_shape=[
            jax.ShapeDtypeStruct((row_count, units), BF16),
            jax.ShapeDtypeStruct((row_count, 2 * units), BF16),
            jax.ShapeDtypeStruct((row_count, width), BF16),
        ],
        scratch_shapes=[pltpu.VMEM((row_count, units), F32)] * 3,
        compiler_params=pltpu.CompilerParams(vmem_limit_bytes=VMEM_LIMIT),
        cost_estimate=pl.CostEstimate(
            flops=2 * 5 * row_count * width * units,
            bytes_accessed=2 * (3 * row_count * width + 3 * width * units),
            transcendentals=row_count * units,
        ),
        name="chunk_pass",
    )(gathered, gathered, gate_w, up_w, down_w)


def weight_kernel(*refs):
    rows_refs, grads_refs = refs[:CHUNKS], refs[CHUNKS : 2 * CHUNKS]
    hidden_refs, both_refs = refs[2 * CHUNKS : 3 * CHUNKS], refs[3 * CHUNKS : 4 * CHUNKS]
    gate_ref, up_ref, down_ref = refs[4 * CHUNKS :]
    units = gate_ref.shape[1]
    inner, outer = None, None
    for c in range(CHUNKS):
        term = dot(rows_refs[c][...], both_refs[c][...], ((0,), (0,)))
        inner = term if inner is None else inner + term
        term = dot(hidden_refs[c][...], grads_refs[c][...], ((0,), (0,)))
        outer = term if outer is None else outer + term
    gate_ref[...] = inner[:, :units].astype(BF16)
    up_ref[...] = inner[:, units:].astype(BF16)
    down_ref[...] = outer.astype(BF16)


def weight_grads(gathered, hidden, both):
    row_count = gathered[0].shape[0]
    width = gathered[0].shape[1] // 2
    units = hidden[0].shape[1]
    tile = 512
    tiles = width // tile
    return pl.pallas_call(
        weight_kernel,
        grid=(tiles,),
        in_specs=[pl.BlockSpec((row_count, tile), lambda j: (0, j))] * CHUNKS
        + [pl.BlockSpec((row_count, tile), lambda j: (0, j + tiles))] * CHUNKS
        + [pl.BlockSpec((row_count, units), lambda j: (0, 0))] * CHUNKS
        + [pl.BlockSpec((row_count, 2 * units), lambda j: (0, 0))] * CHUNKS,
        out_specs=[
            pl.BlockSpec((tile, units), lambda j: (j, 0)),
            pl.BlockSpec((tile, units), lambda j: (j, 0)),
            pl.BlockSpec((units, tile), lambda j: (0, j)),
        ],
        out_shape=[
            jax.ShapeDtypeStruct((width, units), BF16),
            jax.ShapeDtypeStruct((width, units), BF16),
            jax.ShapeDtypeStruct((units, width), BF16),
        ],
        compiler_params=pltpu.CompilerParams(vmem_limit_bytes=VMEM_LIMIT),
        cost_estimate=pl.CostEstimate(
            flops=2 * 3 * CHUNKS * row_count * width * units,
            bytes_accessed=2 * (2 * CHUNKS * row_count * width + 3 * width * units),
            transcendentals=0,
        ),
        name="weight_grads",
    )(*gathered, *gathered, *hidden, *both)


def combine_kernel(table_ref, *refs):
    part_refs, out_ref = refs[:-1], refs[-1]
    part = pl.program_id(0)
    total = None
    for c, part_ref in enumerate(part_refs):
        table = table_ref[c]
        row = lax.broadcasted_iota(jnp.int32, table.shape, 0)
        mine = jnp.where(row % PARTS == part, table, jnp.zeros_like(table))
        term = dot(mine, part_ref[...], ((0,), (0,)))
        total = term if total is None else total + term
    out_ref[...] = total.astype(BF16)


def combine(table, parts):
    folded, width = parts[0].shape
    tok_count = table.shape[2]
    return pl.pallas_call(
        combine_kernel,
        grid=(PARTS,),
        in_specs=[pl.BlockSpec(table.shape, lambda p: (0, 0, 0))]
        + [pl.BlockSpec((folded, width), lambda p: (0, 0))] * CHUNKS,
        out_specs=pl.BlockSpec((tok_count, width), lambda p: (0, p)),
        out_shape=jax.ShapeDtypeStruct((tok_count, width * PARTS), BF16),
        compiler_params=pltpu.CompilerParams(vmem_limit_bytes=VMEM_LIMIT),
        name="combine",
    )(table, *parts)


def exchange(x, experts):
    folded, width = x.shape
    blocks = x.reshape(experts, folded // experts, width)
    return lax.all_to_all(
        blocks, ("grp", "sp"), split_axis=0, concat_axis=0, tiled=True
    ).reshape(folded, width)


def body(tokens, grad_out, expert_ids, gate_codes, lengths, w_gate, w_up, w_down):
    experts = lax.axis_size("grp") * lax.axis_size("sp")
    *sent, table = select_rows(tokens, grad_out, expert_ids, gate_codes, lengths, experts)
    gate_w, up_w, down_w = w_gate[0], w_up[0], w_down[0]
    gathered, hidden, both, parts = [], [], [], []
    for c in range(CHUNKS):
        arrived = unfold(exchange(sent[c], experts))
        gathered.append(lax.all_gather(arrived, "dp", axis=0, tiled=True))
    for c in range(CHUNKS):
        hidden_c, both_c, term = chunk_pass(gathered[c], gate_w, up_w, down_w)
        hidden.append(hidden_c)
        both.append(both_c)
        summed = lax.psum_scatter(term, "dp", scatter_dimension=0, tiled=True)
        parts.append(exchange(fold(summed), experts))
    gate_w_grad, up_w_grad, down_w_grad = weight_grads(gathered, hidden, both)
    grad_tokens = combine(table, parts)
    return (grad_tokens, gate_w_grad[None], up_w_grad[None], down_w_grad[None])


def solution(mesh):
    return jax.shard_map(
        body,
        mesh=mesh,
        in_specs=(
            P(("grp", "dp", "sp"), None),
            P(("grp", "dp", "sp"), None),
            P(("grp", "dp", "sp"), None),
            P(("grp", "dp", "sp"), None),
            P(("grp", "dp", "sp"), None),
            P(("grp", "sp"), None, "dp"),
            P(("grp", "sp"), None, "dp"),
            P(("grp", "sp"), "dp", None),
        ),
        out_specs=(
            P(("grp", "dp", "sp"), None),
            P(("grp", "sp"), None, "dp"),
            P(("grp", "sp"), None, "dp"),
            P(("grp", "sp"), "dp", None),
        ),
        check_vma=False,
    )
```

time: 382 us -> 509 us (1.33)
  waiting for transfers between devices: 187 us -> 348 us
  matrix products: 70.5 us -> 0 us
  Pallas kernels: 0 us -> 69.5 us
  local copies, waits for them, and re-layouts: 65.4 us -> 16.8 us
  starting transfers between devices: 5.7 us -> 20.1 us
    reduce_scatter x1 -> x3, waiting for transfers between devices: 72.6 us -> 203 us  [body(): summed = lax.psum_scatter(term, 'dp', scatter_dimension=0, tiled=True)]
    dot_general x12 -> x0, matrix products: 70.5 us -> none  [the longest x1 13.2 us: hidden_terms(): lax.dot_general(up_piece, up_w, contract_hidden, preferred_element_type=j...]
    pallas_call x0 -> x12, Pallas kernels: none -> 69.5 us  [the longest x3 37.7 us: chunk_pass(): pl.pallas_call(chunk_kernel, grid=(2 * tiles,), in_specs=[pl.BlockSpec((r...]
    all_gather x2 -> x3, waiting for transfers between devices: 108 us -> 145 us  [body(): gathered.append(lax.all_gather(arrived, 'dp', axis=0, tiled=True))]
    reshape x3 -> x0, local copies, waits for them, and re-layouts: 35.2 us -> none  [the longest x1 16.5 us: body(): rows = all_tokens.reshape(-1, width)]
    all_gather x2 -> x0, local copies, waits for them, and re-layouts: 25.9 us -> none  [the longest x1 12.9 us: body(): lax.all_gather(recv_tokens, 'dp', axis=0, tiled=True)]
    unnamed x12 -> x30, local copies, waits for them, and re-layouts: 0.75 us -> 16.8 us
    all_to_all x1 -> x3, starting transfers between devices: 5.4 us -> 19.9 us  [exchange(): lax.all_to_all(blocks, ('grp', 'sp'), split_axis=0, concat_axis=0, tiled=...]
  transfers between devices with their start and end apart: 4 -> 9, of which waited for: 4 -> 6; matrix products, arithmetic and copies ran while one was open for 18% -> 0% of each run, Pallas kernels for 0% -> 12%
where the time goes in v1:
time: 509 us; the launch traced here: 507 us
  waiting for transfers between devices  348 us (68%)
  Pallas kernels  69.5 us (14%)
  blocking collectives  38.4 us (8%)
  starting transfers between devices  20.1 us (4%)
  local copies, waits for them, and re-layouts  16.8 us (3%)
  between operations  14.2 us (3%)
    reduce_scatter x3, waiting for transfers between devices, body(): summed = lax.psum_scatter(term, 'dp', scatter_dimension=0, tiled=True)  203 us
    all_gather x3, waiting for transfers between devices, body(): gathered.append(lax.all_gather(arrived, 'dp', axis=0, tiled=True))  145 us
    all_to_all x3, blocking collectives, exchange(): lax.all_to_all(blocks, ('grp', 'sp'), split_axis=0, concat_axis=0, tiled=...  38.4 us
    pallas_call x3, Pallas kernels, chunk_pass(): pl.pallas_call(chunk_kernel, grid=(2 * tiles,), in_specs=[pl.BlockSpec((r...  37.7 us
    all_to_all x3, starting transfers between devices, exchange(): lax.all_to_all(blocks, ('grp', 'sp'), split_axis=0, concat_axis=0, tiled=...  19.9 us
    unnamed x30, local copies, waits for them, and re-layouts  16.8 us
    pallas_call x1, Pallas kernels, weight_grads(): pl.pallas_call(weight_kernel, grid=(tiles,), in_specs=[pl.BlockSpec((row_...  16 us
  transfers between devices with their start and end apart: 9, of which 6 were waited for; matrix products, arithmetic and copies ran while one was open for 0% of the time, Pallas kernels for 12%

profile of v1, /device:TPU:1, one launch (start us, length us, event | category | flops | bytes accessed | tf_op | source)
XLA Modules:
  0.0 507.3 jit_solution(15701245382124882231)
XLA Ops:
  7.2 0.0 all-gather.4.cloned.1.call-start
  7.2 0.0 copy-start.7
  7.2 1.5 copy-done.7
  8.7 0.0 copy-start.8
  8.7 1.5 copy-done.8
  10.2 0.0 copy-start.12
  10.2 0.7 copy-done.12
  10.9 0.0 copy-start.13
  10.9 0.7 copy-done.13
  11.6 0.0 copy-start.14
  11.6 0.7 copy-done.14
  12.2 3.9 select_rows.1
  16.1 14.3 %all_to_all.30 = bf16[8,8,3584]{2,1,0:T(8,128)(2,1)S(1)} all-to-all(bf16[8,8,3584]{2,1,0:T(8,128)(2,1)S(1)} %bitcast.37), channel_id=1, replica_groups=mesh['grp'=2,'dp'=16,'sp'=4] {'grp','sp'}, dimensions={0} | all-to-all | bytes 917504 | tf_op jit(solution)/shard_map/all_to_all | solution.py:318
  30.4 1.8 unfold.3
  32.3 0.0 all-gather.4.cloned.1.call-update
  32.3 0.0 all-gather.6.cloned.1.call-start
  32.4 11.9 %all_to_all.31 = bf16[8,8,3584]{2,1,0:T(8,128)(2,1)S(1)} all-to-all(bf16[8,8,3584]{2,1,0:T(8,128)(2,1)S(1)} %bitcast.36), channel_id=1, replica_groups=mesh['grp'=2,'dp'=16,'sp'=4] {'grp','sp'}, dimensions={0} | all-to-all | bytes 917504 | tf_op jit(solution)/shard_map/all_to_all | solution.py:318
  44.2 0.0 copy-start
  44.2 1.8 unfold.4
  46.1 0.0 all-gather.6.cloned.1.call-update
  46.1 0.0 all-gather.8.cloned.1.call-start
  46.2 12.3 %all_to_all.32 = bf16[8,8,3584]{2,1,0:T(8,128)(2,1)S(1)} all-to-all(bf16[8,8,3584]{2,1,0:T(8,128)(2,1)S(1)} %bitcast.35), channel_id=1, replica_groups=mesh['grp'=2,'dp'=16,'sp'=4] {'grp','sp'}, dimensions={0} | all-to-all | bytes 917504 | tf_op jit(solution)/shard_map/all_to_all | solution.py:318
  58.4 1.8 unfold.5
  60.3 0.0 all-gather.8.cloned.1.call-update
  60.3 0.0 reduce-scatter.4.cloned.1.call-start
  60.3 39.2 %all-gather.4.cloned.1.call-done.rows_ref.grads_ref.refs_0_.refs_3_ = bf16[256,14336]{1,0:T(8,128)(2,1)} async-done(((bf16[16,14336]{1,0:T(8,128)(2,1)}), bf16[256,14336]{1,0:T(8,128)(2,1)}) %all-gather.4.cloned.1.call-update) | async-done | bytes 7340048 | tf_op jit(solution)/shard_map/all_gather | solution.py:330
  99.5 0.0 copy-done
  99.5 0.0 copy-start.1
  99.5 1.5 copy-done.1
  101.0 0.0 copy-start.4
  101.0 1.5 copy-done.4
  102.5 12.6 %chunk_pass.3 = (bf16[256,128]{1,0:T(8,128)(2,1)S(1)}, bf16[256,256]{1,0:T(8,128)(2,1)S(1)}, bf16[256,7168]{1,0:T(8,128)(2,1)}) custom-call(bf16[256,14336]{1,0:T(8,128)(2,1)} %all-gather.4.cloned.1.call-done.rows_ref.grads_ref.refs_0_.refs_3_, bf16[256,14336]{1,0:T(8,128)(2,1)} %all-gather.4.cloned.1.call-done.rows_ref.grads_ref.refs_0_.refs_3_, ...), custom_call_target="tpu_custom_call" | custom-call | flops 2348810240 | bytes 16515072 | tf_op jit(solution)/shard_map/chunk_pass/pallas_call | solution.py:207
  115.1 0.0 reduce-scatter.4.cloned.1.call-update
  115.1 0.0 reduce-scatter.6.cloned.1.call-start
  115.2 53.0 %all-gather.6.cloned.1.call-done.rows_ref.grads_ref.refs_1_.refs_4_ = bf16[256,14336]{1,0:T(8,128)(2,1)} async-done(((bf16[16,14336]{1,0:T(8,128)(2,1)}), bf16[256,14336]{1,0:T(8,128)(2,1)}) %all-gather.6.cloned.1.call-update) | async-done | bytes 7340048 | tf_op jit(solution)/shard_map/all_gather | solution.py:330
  168.2 0.0 copy-start.2
  168.2 1.5 copy-done.2
  169.7 0.0 copy-start.5
  169.7 1.5 copy-done.5
  171.2 12.6 %chunk_pass.4 = (bf16[256,128]{1,0:T(8,128)(2,1)S(1)}, bf16[256,256]{1,0:T(8,128)(2,1)S(1)}, bf16[256,7168]{1,0:T(8,128)(2,1)}) custom-call(bf16[256,14336]{1,0:T(8,128)(2,1)} %all-gather.6.cloned.1.call-done.rows_ref.grads_ref.refs_1_.refs_4_, bf16[256,14336]{1,0:T(8,128)(2,1)} %all-gather.6.cloned.1.call-done.rows_ref.grads_ref.refs_1_.refs_4_, ...), custom_call_target="tpu_custom_call" | custom-call | flops 2348810240 | bytes 16515072 | tf_op jit(solution)/shard_map/chunk_pass/pallas_call | solution.py:207
  183.8 0.0 reduce-scatter.6.cloned.1.call-update
  183.8 0.0 reduce-scatter.8.cloned.1.call-start
  183.8 53.0 %all-gather.8.cloned.1.call-done.rows_ref.grads_ref.refs_2_.refs_5_ = bf16[256,14336]{1,0:T(8,128)(2,1)} async-done(((bf16[16,14336]{1,0:T(8,128)(2,1)}), bf16[256,14336]{1,0:T(8,128)(2,1)}) %all-gather.8.cloned.1.call-update) | async-done | bytes 7340048 | tf_op jit(solution)/shard_map/all_gather | solution.py:330
  236.8 1.5 copy-done.3
  238.3 1.5 copy-done.6
  239.8 12.5 %chunk_pass.5 = (bf16[256,128]{1,0:T(8,128)(2,1)S(1)}, bf16[256,256]{1,0:T(8,128)(2,1)S(1)}, bf16[256,7168]{1,0:T(8,128)(2,1)}) custom-call(bf16[256,14336]{1,0:T(8,128)(2,1)} %all-gather.8.cloned.1.call-done.rows_ref.grads_ref.refs_2_.refs_5_, bf16[256,14336]{1,0:T(8,128)(2,1)} %all-gather.8.cloned.1.call-done.rows_ref.grads_ref.refs_2_.refs_5_, ...), custom_call_target="tpu_custom_call" | custom-call | flops 2348810240 | bytes 16515072 | tf_op jit(solution)/shard_map/chunk_pass/pallas_call | solution.py:207
  252.3 0.0 reduce-scatter.8.cloned.1.call-update
  252.4 62.2 %reduce-scatter.4.cloned.1.call-done.x_ref = bf16[16,7168]{1,0:T(8,128)(2,1)} async-done(((bf16[256,7168]{1,0:T(8,128)(2,1)}), bf16[16,7168]{1,0:T(8,128)(2,1)}) %reduce-scatter.4.cloned.1.call-update) | async-done | bytes 229392 | tf_op jit(solution)/shard_map/reduce_scatter | solution.py:335
  314.6 0.9 copy-done.9
  315.5 1.1 fold.3
  316.6 6.6 %all-to-all-start.1 = ((bf16[8,8,1792]{2,1,0:T(8,128)(2,1)}), bf16[8,8,1792]{2,1,0:T(8,128)(2,1)S(1)}, u32[]{:S(2)}, u32[]{:S(2)}) async-start(bf16[8,8,1792]{2,1,0:T(8,128)(2,1)} %bitcast.7), calls=%async_computation.2 | async-start | bytes 458752 | tf_op jit(solution)/shard_map/all_to_all | solution.py:318
  323.2 70.4 %reduce-scatter.6.cloned.1.call-done.x_ref = bf16[16,7168]{1,0:T(8,128)(2,1)} async-done(((bf16[256,7168]{1,0:T(8,128)(2,1)}), bf16[16,7168]{1,0:T(8,128)(2,1)}) %reduce-scatter.6.cloned.1.call-update) | async-done | bytes 229392 | tf_op jit(solution)/shard_map/reduce_scatter | solution.py:335
  393.6 0.9 copy-done.10
  394.5 1.1 fold.4
  395.6 0.0 all-to-all-done.1
  395.6 6.6 %all-to-all-start.3 = ((bf16[8,8,1792]{2,1,0:T(8,128)(2,1)}), bf16[8,8,1792]{2,1,0:T(8,128)(2,1)S(1)}, u32[]{:S(2)}, u32[]{:S(2)}) async-start(bf16[8,8,1792]{2,1,0:T(8,128)(2,1)} %bitcast.11), calls=%async_computation.5 | async-start | bytes 458752 | tf_op jit(solution)/shard_map/all_to_all | solution.py:318
  402.2 70.4 %reduce-scatter.8.cloned.1.call-done.x_ref = bf16[16,7168]{1,0:T(8,128)(2,1)} async-done(((bf16[256,7168]{1,0:T(8,128)(2,1)}), bf16[16,7168]{1,0:T(8,128)(2,1)}) %reduce-scatter.8.cloned.1.call-update) | async-done | bytes 229392 | tf_op jit(solution)/shard_map/reduce_scatter | solution.py:335
  472.6 0.9 copy-done.11
  473.5 1.1 fold.5
  474.6 0.0 all-to-all-done.3
  474.6 6.6 %all-to-all-start.5 = ((bf16[8,8,1792]{2,1,0:T(8,128)(2,1)}), bf16[8,8,1792]{2,1,0:T(8,128)(2,1)S(1)}, u32[]{:S(2)}, u32[]{:S(2)}) async-start(bf16[8,8,1792]{2,1,0:T(8,128)(2,1)} %bitcast.15), calls=%async_computation.8 | async-start | bytes 458752 | tf_op jit(solution)/shard_map/all_to_all | solution.py:318
  481.2 16.0 %weight_grads.1 = (bf16[7168,128]{1,0:T(8,128)(2,1)}, bf16[7168,128]{1,0:T(8,128)(2,1)}, bf16[128,7168]{1,0:T(8,128)(2,1)}) custom-call(bf16[256,14336]{1,0:T(8,128)(2,1)} %all-gather.4.cloned.1.call-done.rows_ref.grads_ref.refs_0_.refs_3_, bf16[256,14336]{1,0:T(8,128)(2,1)} %all-gather.6.cloned.1.call-done.rows_ref.grads_ref.refs_1_.refs_4_, ...), custom_call_target="tpu_custom_call" | custom-call | flops 4227858432 | bytes 27525120 | tf_op jit(solution)/shard_map/weight_grads/pallas_call | solution.py:260
  497.2 0.0 all-to-all-done.5
  497.2 3.2 combine.1
  (5 shorter events, 0.0 us)
Async XLA Ops:
  7.2 92.4 %all-gather.4.cloned.1.call-start = ((), (), s32[]{:S(2)}) async-start(), calls=%async_computation.9 | async-start | bytes 7798784 | tf_op jit(solution)/shard_map/all_gather | solution.py:330
  7.2 1.5 copy-start.7
  8.7 1.5 copy-start.8
  10.2 0.7 copy-start.12
  10.9 0.7 copy-start.13
  11.6 0.7 copy-start.14
  32.3 135.9 %all-gather.6.cloned.1.call-start = ((), (), s32[]{:S(2)}) async-start(), calls=%async_computation.11 | async-start | bytes 7798784 | tf_op jit(solution)/shard_map/all_gather | solution.py:330
  44.2 55.3 %copy-start = (bf16[1,7168,128]{2,1,0:T(8,128)(2,1)S(1)}, bf16[1,7168,128]{2,1,0:T(8,128)(2,1)}, u32[]{:S(2)}) copy-start(bf16[1,7168,128]{2,1,0:T(8,128)(2,1)} %param.13) | copy-start | bytes 5505028
  46.1 190.7 %all-gather.8.cloned.1.call-start = ((), (), s32[]{:S(2)}) async-start(), calls=%async_computation.13 | async-start | bytes 7798784 | tf_op jit(solution)/shard_map/all_gather | solution.py:330
  60.3 254.3 %reduce-scatter.4.cloned.1.call-start = ((), (), s32[]{:S(2)}) async-start(), calls=%async_computation.10 | async-start | bytes 3899392 | tf_op jit(solution)/shard_map/reduce_scatter | solution.py:335
  99.5 1.5 copy-start.1
  101.0 1.5 copy-start.4
  115.1 278.5 %reduce-scatter.6.cloned.1.call-start = ((), (), s32[]{:S(2)}) async-start(), calls=%async_computation.12 | async-start | bytes 3899392 | tf_op jit(solution)/shard_map/reduce_scatter | solution.py:335
  168.2 1.5 copy-start.2
  169.7 1.5 copy-start.5
  183.8 288.8 %reduce-scatter.8.cloned.1.call-start = ((), (), s32[]{:S(2)}) async-start(), calls=%async_computation.14 | async-start | bytes 3899392 | tf_op jit(solution)/shard_map/reduce_scatter | solution.py:335
  236.8 1.5 copy-start.3
  238.3 1.5 copy-start.6
  314.6 0.9 copy-start.9
  316.6 79.0 %all-to-all-start.1 = ((bf16[8,8,1792]{2,1,0:T(8,128)(2,1)}), bf16[8,8,1792]{2,1,0:T(8,128)(2,1)S(1)}, u32[]{:S(2)}, u32[]{:S(2)}) async-start(bf16[8,8,1792]{2,1,0:T(8,128)(2,1)} %bitcast.7), calls=%async_computation.2 | async-start | bytes 458752 | tf_op jit(solution)/shard_map/all_to_all | solution.py:318
  393.6 0.9 copy-start.10
  395.6 79.0 %all-to-all-start.3 = ((bf16[8,8,1792]{2,1,0:T(8,128)(2,1)}), bf16[8,8,1792]{2,1,0:T(8,128)(2,1)S(1)}, u32[]{:S(2)}, u32[]{:S(2)}) async-start(bf16[8,8,1792]{2,1,0:T(8,128)(2,1)} %bitcast.11), calls=%async_computation.5 | async-start | bytes 458752 | tf_op jit(solution)/shard_map/all_to_all | solution.py:318
  472.6 0.9 copy-start.11
  474.6 22.6 %all-to-all-start.5 = ((bf16[8,8,1792]{2,1,0:T(8,128)(2,1)}), bf16[8,8,1792]{2,1,0:T(8,128)(2,1)S(1)}, u32[]{:S(2)}, u32[]{:S(2)}) async-start(bf16[8,8,1792]{2,1,0:T(8,128)(2,1)} %bitcast.15), calls=%async_computation.8 | async-start | bytes 458752 | tf_op jit(solution)/shard_map/all_to_all | solution.py:318
Sparse Core Ops, SparseCore 0:
  32.4 67.0 all-gather.3
  102.3 65.8 all-gather.5
  170.9 65.8 all-gather.7
  240.0 74.5 reduce-scatter.3
  317.8 75.7 reduce-scatter.5
  396.8 75.7 reduce-scatter.7

commit v2 on v0

v2 whole, which is shorter than its diff:
```python
import jax
import jax.numpy as jnp
from jax import lax
from jax.experimental import pallas as pl
from jax.experimental.pallas import tpu as pltpu
from jax.sharding import PartitionSpec as P

CAP = 6
SIDE = 4
GRID_SCALE = 2048.0
BF16 = jnp.bfloat16
F32 = jnp.float32
PARAMS = pltpu.CompilerParams(vmem_limit_bytes=48 * 1024 * 1024)
SMEM = pl.BlockSpec(memory_space=pltpu.SMEM)
VMEM = pl.BlockSpec(memory_space=pltpu.VMEM)


def dot(a, b, contract):
    return lax.dot_general(a, b, (contract, ((), ())), preferred_element_type=F32)


NN = ((1,), (0,))
NT = ((1,), (1,))
TN = ((0,), (0,))


def shape(*dims, dtype=BF16):
    return jax.ShapeDtypeStruct(dims, dtype)


def shift(x, along_a, step):
    pairs = []
    for grp in range(2):
        for y in range(SIDE):
            for z in range(SIDE):
                if (grp == 0) == along_a:
                    to = (y, (z + step) % SIDE)
                else:
                    to = ((y + step) % SIDE, z)
                pairs.append(
                    (grp * SIDE * SIDE + y * SIDE + z, grp * SIDE * SIDE + to[0] * SIDE + to[1])
                )
    return lax.ppermute(x, ("grp", "dp"), pairs)


def pack_kernel(quarter_ref, gate_ref, up_ref, down_ref, out_ref):
    units = gate_ref.shape[1]
    out_ref[:, :units] = gate_ref[...]
    out_ref[:, units : 2 * units] = up_ref[...]
    out_ref[:, 2 * units :] = down_ref[...].T


def pack_weights(quarter, gate_w, up_w, down_w):
    width, units = gate_w.shape
    part = width // SIDE
    tile = part // 2
    return pl.pallas_call(
        pack_kernel,
        grid_spec=pltpu.PrefetchScalarGridSpec(
            num_scalar_prefetch=1,
            grid=(2,),
            in_specs=[
                pl.BlockSpec((tile, units), lambda j, q: (q[0] * 2 + j, 0)),
                pl.BlockSpec((tile, units), lambda j, q: (q[0] * 2 + j, 0)),
                pl.BlockSpec((units, tile), lambda j, q: (0, q[0] * 2 + j)),
            ],
            out_specs=pl.BlockSpec((tile, 3 * units), lambda j, q: (j, 0)),
        ),
        out_shape=shape(part, 3 * units),
        compiler_params=PARAMS,
        name="pack_weights",
    )(quarter, gate_w, up_w, down_w)


def select_kernel(lengths_ref, ids_ref, codes_ref, *refs):
    pieces, (out_ref, table_ref, rows_ref, scale_ref) = refs[: 2 * SIDE], refs[2 * SIDE :]
    experts, tok_count = ids_ref.shape
    folded = 2 * SIDE * CAP
    row_count = experts * folded

    @pl.when(pl.program_id(0) == 0)
    def _():
        ids = ids_ref[...]
        codes = codes_ref[...]
        slot_len = tok_count // 2
        position = lax.broadcasted_iota(jnp.int32, (1, tok_count), 1)
        bound = jnp.where(
            position < slot_len, lengths_ref[0, 0], lengths_ref[0, 1] + slot_len
        )
        live = position < bound
        expert = lax.broadcasted_iota(jnp.int32, (experts, tok_count), 0)
        member = jnp.zeros((experts, tok_count), F32)
        gate = jnp.zeros((experts, tok_count), F32)
        for e in range(experts):
            hit = ids == e
            found = jnp.sum(hit.astype(F32), axis=0, keepdims=True)
            code = jnp.sum(jnp.where(hit, codes, 0).astype(F32), axis=0, keepdims=True)
            member = jnp.where(
                jnp.logical_and(expert == e, jnp.logical_and(live, found > 0.0)),
                1.0,
                member,
            )
            gate = jnp.where(expert == e, code / GRID_SCALE, gate)
        earlier = lax.broadcasted_iota(jnp.int32, (tok_count, tok_count), 0)
        later = lax.broadcasted_iota(jnp.int32, (tok_count, tok_count), 1)
        rank = dot(member.astype(BF16), (earlier < later).astype(BF16), NN)
        slot_of = jnp.where(member > 0.0, rank, -1.0)

        def spread(x, times):
            return jnp.broadcast_to(
                x[:, None, :], (experts, times, tok_count)
            ).reshape(experts * times, tok_count)

        row = lax.broadcasted_iota(jnp.int32, (row_count, tok_count), 0)
        chosen = spread(slot_of, folded) == (row % CAP).astype(F32)
        rows_ref[...] = chosen.astype(BF16)
        weight = jnp.sum(
            jnp.where(chosen, spread(gate, folded), 0.0), axis=1, keepdims=True
        )
        is_grad = ((row // CAP) % 2)[:, :1] == 1
        scale_ref[...] = jnp.broadcast_to(jnp.where(is_grad, weight, 1.0), scale_ref.shape)
        row = lax.broadcasted_iota(jnp.int32, table_ref.shape, 0)
        table_ref[...] = (
            spread(slot_of, SIDE * CAP) == (row % CAP).astype(F32)
        ).astype(BF16)

    row = lax.broadcasted_iota(jnp.int32, (row_count, tok_count), 0)
    chosen = rows_ref[...]
    total = None
    for p in range(2 * SIDE):
        mine = jnp.where((row // CAP) % (2 * SIDE) == p, chosen, jnp.zeros_like(chosen))
        term = dot(mine, pieces[p][...], NN)
        total = term if total is None else total + term
    out_ref[...] = (scale_ref[:, :1] * total).astype(BF16)


def select_rows(tokens, grad_out, expert_ids, gate_codes, lengths, experts):
    tok_count, width = tokens.shape
    part = width // SIDE
    steps = 2
    tile = part // steps
    row_count = experts * 2 * SIDE * CAP
    table_rows = experts * SIDE * CAP
    whole = pl.BlockSpec((experts, tok_count), lambda j: (0, 0))
    pieces, piece_specs = [], []
    for q in range(SIDE):
        for array in (tokens, grad_out):
            pieces.append(array)
            piece_specs.append(
                pl.BlockSpec((tok_count, tile), lambda j, q=q: (0, q * steps + j))
            )
    return pl.pallas_call(
        select_kernel,
        grid=(steps,),
        in_specs=[SMEM, whole, whole] + piece_specs,
        out_specs=[
            pl.BlockSpec((row_count, tile), lambda j: (0, j)),
            pl.BlockSpec((table_rows, tok_count), lambda j: (0, 0)),
        ],
        out_shape=[shape(row_count, part), shape(table_rows, tok_count)],
        scratch_shapes=[
            pltpu.VMEM((row_count, tok_count), BF16),
            pltpu.VMEM((row_count, 128), F32),
        ],
        compiler_params=PARAMS,
        name="select_rows",
    )(lengths, expert_ids.T, gate_codes.T, *pieces)


def exchange(x, experts):
    folded, width = x.shape
    blocks = x.reshape(experts, folded // experts, width)
    return lax.all_to_all(
        blocks, ("grp", "sp"), split_axis=0, concat_axis=0, tiled=True
    ).reshape(folded, width)


def unfold_kernel(a_ref, x_ref, *out_refs):
    rows, folded = out_refs[0].shape[0], x_ref.shape[0]
    part = x_ref.shape[1]
    to = lax.broadcasted_iota(jnp.int32, (rows, folded), 0)
    src = lax.broadcasted_iota(jnp.int32, (rows, folded), 1)
    first = (to // CAP) * (2 * SIDE * CAP) + to % CAP
    for d, out_ref in enumerate(out_refs):
        quarter = (a_ref[0] + d) % SIDE
        for array in range(2):
            pick = (src == first + (quarter * 2 + array) * CAP).astype(BF16)
            out_ref[:, array * part : (array + 1) * part] = dot(
                pick, x_ref[...], NN
            ).astype(BF16)


def unfold(a, x):
    folded, part = x.shape
    rows = folded // (2 * SIDE)
    return pl.pallas_call(
        unfold_kernel,
        in_specs=[SMEM, VMEM],
        out_shape=[shape(rows, 2 * part)] * SIDE,
        compiler_params=PARAMS,
        name="unfold",
    )(a, x)


def line_kernel(a_ref, *refs):
    out_ref = refs[-1]
    for d, x_ref in enumerate(refs[:-1]):
        rows = x_ref.shape[0]
        at = ((a_ref[0] + SIDE - d) % SIDE) * rows
        out_ref[pl.ds(pl.multiple_of(at, 16), rows), :] = x_ref[...]


def line_up(a, blocks):
    rows, width = blocks[0].shape
    return pl.pallas_call(
        line_kernel,
        in_specs=[SMEM] + [VMEM] * SIDE,
        out_shape=shape(SIDE * rows, width),
        compiler_params=PARAMS,
        name="line_up",
    )(a, *blocks)


def forward_kernel(*refs):
    pieces, weights, outs = refs[:-2 * SIDE], refs[-2 * SIDE : -SIDE], refs[-SIDE:]
    part = weights[0].shape[0]
    units = weights[0].shape[1] // 3
    rows = pieces[0].shape[0]
    for i, piece in enumerate(pieces):
        span = slice(i * rows, (i + 1) * rows)
        for weight, out in zip(weights, outs):
            inner = dot(piece[:, :part], weight[:, : 2 * units], NN)
            out[span, : 2 * units] = inner.astype(out.dtype)
            outer = dot(piece[:, part:], weight[:, 2 * units :], NN)
            out[span, 2 * units :] = outer.astype(out.dtype)


def forward(pieces, weights):
    rows = pieces[0].shape[0] * len(pieces)
    part, columns = weights[0].shape
    return pl.pallas_call(
        forward_kernel,
        in_specs=[VMEM] * (len(pieces) + SIDE),
        out_shape=[shape(rows, columns, dtype=F32)] + [shape(rows, columns)] * (SIDE - 1),
        compiler_params=PARAMS,
        cost_estimate=pl.CostEstimate(
            flops=2 * SIDE * rows * part * columns,
            bytes_accessed=4 * rows * part + 2 * SIDE * (part + rows) * columns,
            transcendentals=0,
        ),
        name="forward",
    )(*pieces, *weights)


def activate_kernel(*refs):
    terms, out_ref = refs[:-1], refs[-1]
    total = terms[0][...]
    for term in terms[1:]:
        total = total + term[...].astype(F32)
    units = total.shape[1] // 3
    gate_pre, up_pre, hidden_grad = (
        total[:, :units], total[:, units : 2 * units], total[:, 2 * units :],
    )
    logistic = 1.0 / (1.0 + jnp.exp(-gate_pre))
    out_ref[:, :units] = (gate_pre * logistic * up_pre).astype(BF16)
    out_ref[:, units : 2 * units] = (
        hidden_grad * up_pre * logistic * (1.0 + gate_pre * (1.0 - logistic))
    ).astype(BF16)
    out_ref[:, 2 * units :] = (hidden_grad * gate_pre * logistic).astype(BF16)


def activate(terms):
    return pl.pallas_call(
        activate_kernel,
        in_specs=[VMEM] * SIDE,
        out_shape=shape(*terms[0].shape),
        compiler_params=PARAMS,
        name="activate",
    )(*terms)


def backward_kernel(*refs):
    hidden, weights, outs = refs[:SIDE], refs[SIDE : 2 * SIDE], refs[2 * SIDE :]
    rows = outs[0].shape[0]
    units = hidden[0].shape[1] // 3
    for i, out in enumerate(outs):
        span = slice(i * rows, (i + 1) * rows)
        total = None
        for h, weight in zip(hidden, weights):
            term = dot(h[span, units:], weight[:, : 2 * units], NT)
            total = term if total is None else total + term
        out[...] = total.astype(out.dtype)


def backward(hidden, weights, dtypes):
    rows = hidden[0].shape[0] // len(dtypes)
    part, columns = weights[0].shape
    return pl.pallas_call(
        backward_kernel,
        in_specs=[VMEM] * (2 * SIDE),
        out_shape=[shape(rows, part, dtype=dtype) for dtype in dtypes],
        compiler_params=PARAMS,
        cost_estimate=pl.CostEstimate(
            flops=2 * SIDE * rows * len(dtypes) * part * columns * 2 // 3,
            bytes_accessed=2 * SIDE * (part + rows * len(dtypes)) * columns,
            transcendentals=0,
        ),
        name="backward",
    )(*hidden, *weights)


def weight_kernel(*refs):
    pieces, hidden, out_ref = refs[:SIDE], refs[SIDE:-1], refs[-1]
    part = out_ref.shape[0]
    units = out_ref.shape[1] // 3
    rows = pieces[0].shape[0]
    inner, outer, i = None, None, 0
    for h in hidden:
        for k in range(h.shape[0] // rows):
            span = slice(k * rows, (k + 1) * rows)
            piece = pieces[i]
            term = dot(piece[:, :part], h[span, units:], TN)
            inner = term if inner is None else inner + term
            term = dot(piece[:, part:], h[span, :units], TN)
            outer = term if outer is None else outer + term
            i += 1
    out_ref[:, : 2 * units] = inner.astype(BF16)
    out_ref[:, 2 * units :] = outer.astype(BF16)


def weight_grads(pieces, hidden):
    part = pieces[0].shape[1] // 2
    columns = hidden[0].shape[1]
    rows = pieces[0].shape[0] * SIDE
    return pl.pallas_call(
        weight_kernel,
        in_specs=[VMEM] * (SIDE + len(hidden)),
        out_shape=shape(part, columns),
        compiler_params=PARAMS,
        cost_estimate=pl.CostEstimate(
            flops=2 * rows * part * columns,
            bytes_accessed=4 * rows * part + 2 * (part + rows) * columns,
            transcendentals=0,
        ),
        name="weight_grads",
    )(*pieces, *hidden)


def unpack_kernel(quarter_ref, x_ref, *refs):
    gate_ref, up_ref, down_ref = refs[-3:]
    units = gate_ref.shape[1]
    gate_ref[...] = x_ref[:, :units]
    up_ref[...] = x_ref[:, units : 2 * units]
    down_ref[...] = x_ref[:, 2 * units :].T


def unpack(quarter, x, into):
    part, columns = x.shape
    units, width = columns // 3, part * SIDE
    tile = part // 2
    earlier = [] if into is None else list(into)
    return pl.pallas_call(
        unpack_kernel,
        grid_spec=pltpu.PrefetchScalarGridSpec(
            num_scalar_prefetch=1,
            grid=(2,),
            in_specs=[pl.BlockSpec((tile, columns), lambda j, q: (j, 0))]
            + [pl.BlockSpec(memory_space=pl.ANY)] * len(earlier),
            out_specs=[
                pl.BlockSpec((tile, units), lambda j, q: (q[0] * 2 + j, 0)),
                pl.BlockSpec((tile, units), lambda j, q: (q[0] * 2 + j, 0)),
                pl.BlockSpec((units, tile), lambda j, q: (0, q[0] * 2 + j)),
            ],
        ),
        out_shape=[shape(width, units), shape(width, units), shape(units, width)],
        input_output_aliases={2 + i: i for i in range(len(earlier))},
        compiler_params=PARAMS,
        name="unpack",
    )(quarter, x, *earlier)


def sum_kernel(a_ref, *refs):
    terms, outs = refs[:SIDE], refs[SIDE:]
    rows = outs[0].shape[0]
    for d, out in enumerate(outs):
        at = pl.multiple_of(((a_ref[0] + d) % SIDE) * rows, 16)
        total = None
        for term in terms:
            x = term[pl.ds(at, rows), :].astype(F32)
            total = x if total is None else total + x
        out[...] = total.astype(BF16)


def sum_rows(a, terms):
    rows, part = terms[0].shape
    return pl.pallas_call(
        sum_kernel,
        in_specs=[SMEM] + [VMEM] * SIDE,
        out_shape=[shape(rows // SIDE, part)] * SIDE,
        compiler_params=PARAMS,
        name="sum_rows",
    )(a, *terms)


def fold_kernel(a_ref, *refs):
    out_ref = refs[-1]
    folded, rows = out_ref.shape[0], refs[0].shape[0]
    to = lax.broadcasted_iota(jnp.int32, (folded, rows), 0)
    src = lax.broadcasted_iota(jnp.int32, (folded, rows), 1)
    first = (src // CAP) * (SIDE * CAP) + src % CAP
    total = None
    for d, x_ref in enumerate(refs[:-1]):
        quarter = (a_ref[0] + SIDE - d) % SIDE
        term = dot((to == first + quarter * CAP).astype(BF16), x_ref[...], NN)
        total = term if total is None else total + term
    out_ref[...] = total.astype(BF16)


def fold(a, blocks):
    rows, part = blocks[0].shape
    return pl.pallas_call(
        fold_kernel,
        in_specs=[SMEM] + [VMEM] * SIDE,
        out_shape=shape(rows * SIDE, part),
        compiler_params=PARAMS,
        name="fold",
    )(a, *blocks)


def combine_kernel(table_ref, x_ref, out_ref):
    table = table_ref[...]
    row = lax.broadcasted_iota(jnp.int32, table.shape, 0)
    quarter = pl.program_id(0)
    mine = jnp.where((row // CAP) % SIDE == quarter, table, jnp.zeros_like(table))
    out_ref[...] = dot(mine, x_ref[...], TN).astype(BF16)


def combine(table, x):
    folded, part = x.shape
    tok_count = table.shape[1]
    return pl.pallas_call(
        combine_kernel,
        grid=(SIDE,),
        in_specs=[
            pl.BlockSpec(table.shape, lambda q: (0, 0)),
            pl.BlockSpec((folded, part), lambda q: (0, 0)),
        ],
        out_specs=pl.BlockSpec((tok_count, part), lambda q: (0, q)),
        out_shape=shape(tok_count, part * SIDE),
        compiler_params=PARAMS,
        name="combine",
    )(table, x)


def body(tokens, grad_out, expert_ids, gate_codes, lengths, w_gate, w_up, w_down):
    experts = lax.axis_size("grp") * lax.axis_size("sp")
    dp = lax.axis_index("dp")
    a = jnp.where(lax.axis_index("grp") == 0, dp % SIDE, dp // SIDE).astype(jnp.int32)[None]
    quarters = [(a + d) % SIDE for d in range(SIDE)]
    gate_w, up_w, down_w = w_gate[0], w_up[0], w_down[0]

    weights = [pack_weights(quarters[d], gate_w, up_w, down_w) for d in range(SIDE)]
    weights = [weights[0]] + [shift(weights[d], True, d) for d in range(1, SIDE)]

    sent, table = select_rows(tokens, grad_out, expert_ids, gate_codes, lengths, experts)
    blocks = unfold(a, exchange(sent, experts))
    blocks = [blocks[0]] + [shift(blocks[d], True, d) for d in range(1, SIDE)]
    line = line_up(a, blocks)
    steps = (0, 1, -1, 2)
    pieces = [line] + [shift(line, False, step) for step in steps[1:]]

    terms = forward(pieces, weights)
    terms = [terms[0]] + [shift(terms[d], True, -d) for d in range(1, SIDE)]
    acts = activate(terms)
    hidden = [acts] + [shift(acts, True, d) for d in range(1, SIDE)]

    row_terms = backward(hidden, weights, [F32, BF16, BF16, BF16])
    row_terms = [row_terms[0]] + [
        shift(row_terms[i], False, -steps[i]) for i in range(1, SIDE)
    ]
    parts = sum_rows(a, row_terms)
    parts = [parts[0]] + [shift(parts[d], True, d) for d in range(1, SIDE)]
    grad_tokens = combine(table, exchange(fold(a, parts), experts))

    order = (1, 3, 2, 0)
    grads = {d: weight_grads(pieces, [hidden[d]]) for d in order}
    grads = {d: shift(grads[d], True, -d) if d else grads[d] for d in order}
    into = None
    for d in (0, 1, 3, 2):
        into = unpack(quarters[d], grads[d], into)
    gate_w_grad, up_w_grad, down_w_grad = into
    return (grad_tokens, gate_w_grad[None], up_w_grad[None], down_w_grad[None])


def solution(mesh):
    return jax.shard_map(
        body,
        mesh=mesh,
        in_specs=(
            P(("grp", "dp", "sp"), None),
            P(("grp", "dp", "sp"), None),
            P(("grp", "dp", "sp"), None),
            P(("grp", "dp", "sp"), None),
            P(("grp", "dp", "sp"), None),
            P(("grp", "sp"), None, "dp"),
            P(("grp", "sp"), None, "dp"),
            P(("grp", "sp"), "dp", None),
        ),
        out_specs=(
            P(("grp", "dp", "sp"), None),
            P(("grp", "sp"), None, "dp"),
            P(("grp", "sp"), None, "dp"),
            P(("grp", "sp"), "dp", None),
        ),
        check_vma=False,
    )
```

time: 382 us -> 251 us (0.66)
  matrix products: 70.5 us -> 0 us
  Pallas kernels: 0 us -> 59.3 us
  local copies, waits for them, and re-layouts: 65.4 us -> 14.5 us
  waiting for transfers between devices: 187 us -> 139 us
  blocking collectives: 36.4 us -> 0 us
  starting transfers between devices: 5.7 us -> 36.5 us
  between operations: 13.9 us -> 0.83 us
    ppermute x0 -> x24, waiting for transfers between devices: none -> 125 us  [shift(): return lax.ppermute(x, ('grp', 'dp'), pairs)]
    all_gather x2 -> x0, waiting for transfers between devices: 108 us -> none  [the longest x1 62.6 us: body(): lax.all_gather(recv_tokens, 'dp', axis=0, tiled=True)]
    reduce_scatter x1 -> x0, waiting for transfers between devices: 72.6 us -> none  [body(): lax.psum_scatter(hidden_terms(gate_grad, up_grad, gate_w, up_w).astype(jn...]
    dot_general x12 -> x0, matrix products: 70.5 us -> none  [the longest x1 13.2 us: hidden_terms(): lax.dot_general(up_piece, up_w, contract_hidden, preferred_element_type=j...]
    pallas_call x0 -> x21, Pallas kernels: none -> 59.3 us  [the longest x4 17.2 us: weight_grads(): pl.pallas_call(weight_kernel, in_specs=[VMEM] * (SIDE + len(hidden)), out...]
    all_to_all x2 -> x0, blocking collectives: 36.4 us -> none  [the longest x1 19.2 us: body(): lax.all_to_all(sent_tokens, ('grp', 'sp'), split_axis=0, concat_axis=0, t...]
    reshape x3 -> x0, local copies, waits for them, and re-layouts: 35.2 us -> none  [the longest x1 16.5 us: body(): rows = all_tokens.reshape(-1, width)]
    ppermute x0 -> x24, starting transfers between devices: none -> 26.6 us  [shift(): return lax.ppermute(x, ('grp', 'dp'), pairs)]
  transfers between devices with their start and end apart: 4 -> 26, of which waited for: 4 -> 13; matrix products, arithmetic and copies ran while one was open for 18% -> 0% of each run, Pallas kernels for 0% -> 14%
where the time goes in v2:
time: 251 us; the launch traced here: 250 us
  waiting for transfers between devices  139 us (55%)
  Pallas kernels  59.3 us (24%)
  starting transfers between devices  36.5 us (15%)
  local copies, waits for them, and re-layouts  14.5 us (6%)
    ppermute x24, waiting for transfers between devices, shift(): return lax.ppermute(x, ('grp', 'dp'), pairs)  125 us
    ppermute x24, starting transfers between devices, shift(): return lax.ppermute(x, ('grp', 'dp'), pairs)  26.6 us
    pallas_call x4, Pallas kernels, weight_grads(): pl.pallas_call(weight_kernel, in_specs=[VMEM] * (SIDE + len(hidden)), out...  17.2 us
    unnamed x38, local copies, waits for them, and re-layouts  14.5 us
    all_to_all x2, waiting for transfers between devices, exchange(): lax.all_to_all(blocks, ('grp', 'sp'), split_axis=0, concat_axis=0, tiled=...  14 us
    all_to_all x2, starting transfers between devices, exchange(): lax.all_to_all(blocks, ('grp', 'sp'), split_axis=0, concat_axis=0, tiled=...  9.98 us
    pallas_call x1, Pallas kernels, forward(): pl.pallas_call(forward_kernel, in_specs=[VMEM] * (len(pieces) + SIDE), ou...  9.77 us
    pallas_call x4, Pallas kernels, unpack(): pl.pallas_call(unpack_kernel, grid_spec=pltpu.PrefetchScalarGridSpec(num_...  7.93 us
  transfers between devices with their start and end apart: 26, of which 13 were waited for; matrix products, arithmetic and copies ran while one was open for 0% of the time, Pallas kernels for 14%

profile of v2, /device:TPU:1, one launch (start us, length us, event | category | flops | bytes accessed | tf_op | source)
XLA Modules:
  0.0 249.9 jit_solution(4332547685711910217)
XLA Ops:
  0.6 1.5 copy-done.4
  2.1 1.5 copy-done.5
  3.6 0.7 copy-done.15
  4.3 0.7 copy-done.16
  5.0 0.7 copy-done.17
  5.7 4.4 %select_rows.1 = (bf16[384,1792]{1,0:T(8,128)(2,1)S(1)}, bf16[192,128]{1,0:T(8,128)(2,1)S(1)}) custom-call(s32[1,2]{1,0:T(1,128)S(1)} %copy-done.17, s32[8,128]{1,0:T(8,128)S(1)} %bitcast.25, s32[8,128]{1,0:T(8,128)S(1)} %bitcast.26, bf16[128,7168]{1,0:T(8,128)(2,1)S(1)} %copy-done.4, bf16[128,7168]{1,0:T(8,128)(2,1)S(1)} %copy-done.5, ...), custom_call_target="tpu_custom_call" | custom-call | tf_op jit(solution)/shard_map/select_rows/pallas_call | solution.py:152
  10.1 1.1 copy-done.13
  11.1 5.9 %all-to-all-start = ((bf16[8,48,1792]{2,1,0:T(8,128)(2,1)}), bf16[8,48,1792]{2,1,0:T(8,128)(2,1)S(1)}, u32[]{:S(2)}, u32[]{:S(2)}) async-start(bf16[8,48,1792]{2,1,0:T(8,128)(2,1)} %bitcast.24), calls=%async_computation | async-start | bytes 2752512 | tf_op jit(solution)/shard_map/all_to_all | solution.py:173
  17.1 1.5 copy-done.1
  18.6 2.1 pack_weights.5
  20.7 1.3 collective-permute-start.6
  22.0 14.0 %all-to-all-done = bf16[8,48,1792]{2,1,0:T(8,128)(2,1)S(1)} async-done(((bf16[8,48,1792]{2,1,0:T(8,128)(2,1)}), bf16[8,48,1792]{2,1,0:T(8,128)(2,1)S(1)}, u32[]{:S(2)}, u32[]{:S(2)}) %all-to-all-start) | async-done | bytes 1376288 | tf_op jit(solution)/shard_map/all_to_all | solution.py:173
  36.0 2.0 unfold.1
  38.0 1.4 collective-permute-start
  39.4 2.6 %collective-permute-start.1 = (bf16[48,3584]{1,0:T(8,128)(2,1)S(1)}, bf16[48,3584]{1,0:T(8,128)(2,1)S(1)}, u32[]{:S(2)}, u32[]{:S(2)}) collective-permute-start(bf16[48,3584]{1,0:T(8,128)(2,1)S(1)} %get-tuple-element.38), channel_id=1, source_target_pairs={{0,8},{4,12},{8,0},{12,4},{16,24},{20,28},{24,16},{28,20},{32,40},... | collective-permute-start | bytes 1032200 | tf_op jit(solution)/shard_map/ppermute | solution.py:43
  42.0 1.1 collective-permute-start.2
  43.1 1.5 copy-done.2
  44.6 1.3 pack_weights.6
  46.2 1.3 pack_weights.7
  47.6 2.7 %collective-permute-start.8 = (bf16[1792,384]{1,0:T(8,128)(2,1)S(1)}, bf16[1792,384]{1,0:T(8,128)(2,1)}, u32[]{:S(2)}, u32[]{:S(2)}) collective-permute-start(bf16[1792,384]{1,0:T(8,128)(2,1)S(1)} %pack_weights.7), channel_id=1, source_target_pairs={{0,12},{4,0},{8,4},{12,8},{16,28},{20,16},{24,20},{28,24},{32,44},... | collective-permute-start | bytes 4128776 | tf_op jit(solution)/shard_map/ppermute | solution.py:43
  50.2 0.4 collective-permute-done.1.refs_2_
  50.7 3.0 %collective-permute-start.5 = (bf16[192,3584]{1,0:T(8,128)(2,1)S(1)}, bf16[192,3584]{1,0:T(8,128)(2,1)S(1)}, u32[]{:S(2)}, u32[]{:S(2)}) collective-permute-start(bf16[192,3584]{1,0:T(8,128)(2,1)S(1)} %line_up.1.refs_0_), channel_id=1, source_target_pairs={{0,32},{4,36},{8,40},{12,44},{16,48},{20,52},{24,56},{28,60},{32,0... | collective-permute-start | bytes 4128776 | tf_op jit(solution)/shard_map/ppermute | solution.py:43
  53.7 0.6 collective-permute-start.4
  54.4 0.8 collective-permute-start.3
  55.2 1.3 pack_weights.4.refs_4_
  56.5 1.1 copy-done.14
  57.6 15.7 %collective-permute-done.7.refs_6_ = bf16[1792,384]{1,0:T(8,128)(2,1)} collective-permute-done((bf16[1792,384]{1,0:T(8,128)(2,1)S(1)}, bf16[1792,384]{1,0:T(8,128)(2,1)}, u32[]{:S(2)}, u32[]{:S(2)}) %collective-permute-start.7) | collective-permute-done | bytes 1376288 | tf_op jit(solution)/shard_map/ppermute | solution.py:43
  73.3 34.7 %collective-permute-done.8.refs_7_ = bf16[1792,384]{1,0:T(8,128)(2,1)} collective-permute-done((bf16[1792,384]{1,0:T(8,128)(2,1)S(1)}, bf16[1792,384]{1,0:T(8,128)(2,1)}, u32[]{:S(2)}, u32[]{:S(2)}) %collective-permute-start.8) | collective-permute-done | bytes 1376288 | tf_op jit(solution)/shard_map/ppermute | solution.py:43
  108.0 2.3 collective-permute-done.4.refs_2_
  110.3 1.1 copy-done.6
  111.4 9.8 %forward.1 = (f32[768,384]{1,0:T(8,128)S(1)}, bf16[768,384]{1,0:T(8,128)(2,1)S(1)}, bf16[768,384]{1,0:T(8,128)(2,1)S(1)}, bf16[768,384]{1,0:T(8,128)(2,1)S(1)}) custom-call(bf16[192,3584]{1,0:T(8,128)(2,1)S(1)} %line_up.1.refs_0_, bf16[192,3584]{1,0:T(8,128)(2,1)S(1)} %collective-permute-done.3.refs_1_, bf16[192,3584]{1,0:T(8,128)(2,1)} %copy-done.6, ...), custom_call_target="tpu_custom_call" | custom-call | flops 4227858432 | bytes 13369344 | tf_op jit(solution)/shard_map/forward/pallas_call | solution.py:241
  121.1 5.4 %collective-permute-start.9 = (bf16[768,384]{1,0:T(8,128)(2,1)S(1)}, bf16[768,384]{1,0:T(8,128)(2,1)S(1)}, u32[]{:S(2)}, u32[]{:S(2)}) collective-permute-start(bf16[768,384]{1,0:T(8,128)(2,1)S(1)} %get-tuple-element.41), channel_id=1, source_target_pairs={{0,12},{4,0},{8,4},{12,8},{16,28},{20,16},{24,20},{28,24},{32,44},... | collective-permute-start | bytes 1769480 | tf_op jit(solution)/shard_map/ppermute | solution.py:43
  126.5 0.7 collective-permute-start.11
  127.2 12.5 %collective-permute-done.9.refs_1_ = bf16[768,384]{1,0:T(8,128)(2,1)S(1)} collective-permute-done((bf16[768,384]{1,0:T(8,128)(2,1)S(1)}, bf16[768,384]{1,0:T(8,128)(2,1)S(1)}, u32[]{:S(2)}, u32[]{:S(2)}) %collective-permute-start.9) | collective-permute-done | bytes 589856 | tf_op jit(solution)/shard_map/ppermute | solution.py:43
  139.7 3.1 %collective-permute-done.11.refs_3_ = bf16[768,384]{1,0:T(8,128)(2,1)S(1)} collective-permute-done((bf16[768,384]{1,0:T(8,128)(2,1)S(1)}, bf16[768,384]{1,0:T(8,128)(2,1)S(1)}, u32[]{:S(2)}, u32[]{:S(2)}) %collective-permute-start.11) | collective-permute-done | bytes 589856 | tf_op jit(solution)/shard_map/ppermute | solution.py:43
  142.8 0.5 activate.1.refs_0_.refs_4_
  143.3 0.8 collective-permute-start.14
  144.3 0.6 collective-permute-start.12
  144.8 7.6 %collective-permute-done.14.refs_3_.refs_4_ = bf16[768,384]{1,0:T(8,128)(2,1)S(1)} collective-permute-done((bf16[768,384]{1,0:T(8,128)(2,1)S(1)}, bf16[768,384]{1,0:T(8,128)(2,1)S(1)}, u32[]{:S(2)}, u32[]{:S(2)}) %collective-permute-start.14) | collective-permute-done | bytes 589856 | tf_op jit(solution)/shard_map/ppermute | solution.py:43
  152.4 2.3 collective-permute-done.13.refs_2_.refs_4_
  154.6 6.3 %collective-permute-done.12.refs_1_.refs_4_ = bf16[768,384]{1,0:T(8,128)(2,1)S(1)} collective-permute-done((bf16[768,384]{1,0:T(8,128)(2,1)S(1)}, bf16[768,384]{1,0:T(8,128)(2,1)S(1)}, u32[]{:S(2)}, u32[]{:S(2)}) %collective-permute-start.12) | collective-permute-done | bytes 589856 | tf_op jit(solution)/shard_map/ppermute | solution.py:43
  160.9 7.5 %backward.1 = (f32[192,1792]{1,0:T(8,128)S(1)}, bf16[192,1792]{1,0:T(8,128)(2,1)S(1)}, bf16[192,1792]{1,0:T(8,128)(2,1)S(1)}, bf16[192,1792]{1,0:T(8,128)(2,1)S(1)}) custom-call(bf16[768,384]{1,0:T(8,128)(2,1)S(1)} %activate.1.refs_0_.refs_4_, bf16[768,384]{1,0:T(8,128)(2,1)S(1)} %collective-permute-done.12.refs_1_.refs_4_, ...), custom_call_target="tpu_custom_call" | custom-call | flops 2818572288 | bytes 7864320 | tf_op jit(solution)/shard_map/backward/pallas_call | solution.py:298
  168.4 2.2 collective-permute-start.15
  170.6 1.3 collective-permute-start.17
  171.9 4.6 %weight_grads.6 = bf16[1792,384]{1,0:T(8,128)(2,1)} custom-call(bf16[192,3584]{1,0:T(8,128)(2,1)S(1)} %line_up.1.refs_0_, bf16[192,3584]{1,0:T(8,128)(2,1)S(1)} %collective-permute-done.3.refs_1_, bf16[192,3584]{1,0:T(8,128)(2,1)S(1)} %copy-done.7, bf16[192,3584]{1,0:T(8,128)(2,1)} %copy-done.18, bf16[768,384]{1,0:T(8,128)(2,1)S(1)} %collective-permute-done.12.refs_1_.refs_4_), custom_call_target="tpu_custom_call" | custom-call | flops 1056964608 | bytes 7471104 | tf_op jit(solution)/shard_map/weight_grads/pallas_call | solution.py:335
  176.5 0.3 collective-permute-start.23
  176.8 4.6 %weight_grads.5 = bf16[1792,384]{1,0:T(8,128)(2,1)} custom-call(bf16[192,3584]{1,0:T(8,128)(2,1)S(1)} %line_up.1.refs_0_, bf16[192,3584]{1,0:T(8,128)(2,1)S(1)} %collective-permute-done.3.refs_1_, bf16[192,3584]{1,0:T(8,128)(2,1)S(1)} %copy-done.7, bf16[192,3584]{1,0:T(8,128)(2,1)} %copy-done.18, bf16[768,384]{1,0:T(8,128)(2,1)S(1)} %collective-permute-done.14.refs_3_.refs_4_), custom_call_target="tpu_custom_call" | custom-call | flops 1056964608 | bytes 7471104 | tf_op jit(solution)/shard_map/weight_grads/pallas_call | solution.py:335
  181.4 1.1 collective-permute-start.22
  182.5 4.6 %weight_grads.4 = bf16[1792,384]{1,0:T(8,128)(2,1)} custom-call(bf16[192,3584]{1,0:T(8,128)(2,1)S(1)} %line_up.1.refs_0_, bf16[192,3584]{1,0:T(8,128)(2,1)S(1)} %collective-permute-done.3.refs_1_, bf16[192,3584]{1,0:T(8,128)(2,1)S(1)} %copy-done.7, bf16[192,3584]{1,0:T(8,128)(2,1)} %copy-done.18, bf16[768,384]{1,0:T(8,128)(2,1)S(1)} %collective-permute-done.13.refs_2_.refs_4_), custom_call_target="tpu_custom_call" | custom-call | flops 1056964608 | bytes 7471104 | tf_op jit(solution)/shard_map/weight_grads/pallas_call | solution.py:335
  187.1 3.5 %collective-permute-done.16.refs_2_ = bf16[192,1792]{1,0:T(8,128)(2,1)S(1)} collective-permute-done((bf16[192,1792]{1,0:T(8,128)(2,1)S(1)}, bf16[192,1792]{1,0:T(8,128)(2,1)S(1)}, u32[]{:S(2)}, u32[]{:S(2)}) %collective-permute-start.16) | collective-permute-done | bytes 688160 | tf_op jit(solution)/shard_map/ppermute | solution.py:43
  190.7 0.3 sum_rows.1
  191.3 31.9 %collective-permute-done.18.refs_1_ = bf16[48,1792]{1,0:T(8,128)(2,1)S(1)} collective-permute-done((bf16[48,1792]{1,0:T(8,128)(2,1)S(1)}, bf16[48,1792]{1,0:T(8,128)(2,1)S(1)}, u32[]{:S(2)}, u32[]{:S(2)}) %collective-permute-start.18) | collective-permute-done | bytes 172064 | tf_op jit(solution)/shard_map/ppermute | solution.py:43
  223.2 4.5 %collective-permute-done.20.refs_3_ = bf16[48,1792]{1,0:T(8,128)(2,1)S(1)} collective-permute-done((bf16[48,1792]{1,0:T(8,128)(2,1)S(1)}, bf16[48,1792]{1,0:T(8,128)(2,1)S(1)}, u32[]{:S(2)}, u32[]{:S(2)}) %collective-permute-start.20) | collective-permute-done | bytes 172064 | tf_op jit(solution)/shard_map/ppermute | solution.py:43
  227.7 0.8 fold.1
  228.6 0.9 copy-done.10
  229.4 4.0 %all-to-all-start.1 = ((bf16[8,24,1792]{2,1,0:T(8,128)(2,1)}), bf16[8,24,1792]{2,1,0:T(8,128)(2,1)S(1)}, u32[]{:S(2)}, u32[]{:S(2)}) async-start(bf16[8,24,1792]{2,1,0:T(8,128)(2,1)} %bitcast.23), calls=%async_computation.1 | async-start | bytes 1376256 | tf_op jit(solution)/shard_map/all_to_all | solution.py:173
  233.5 1.3 copy-done.9
  234.8 1.1 copy-done.12
  235.9 3.5 %weight_grads.7.x_ref = bf16[1792,384]{1,0:T(8,128)(2,1)S(1)} custom-call(bf16[192,3584]{1,0:T(8,128)(2,1)S(1)} %line_up.1.refs_0_, bf16[192,3584]{1,0:T(8,128)(2,1)S(1)} %copy-done.9, bf16[192,3584]{1,0:T(8,128)(2,1)S(1)} %copy-done.7, bf16[192,3584]{1,0:T(8,128)(2,1)} %copy-done.18, bf16[768,384]{1,0:T(8,128)(2,1)S(1)} %copy-done.12), custom_call_target="tpu_custom_call" | custom-call | flops 1056964608 | bytes 7471104 | tf_op jit(solution)/shard_map/weight_grads/pallas_call | solution.py:335
  239.4 1.2 unpack.4
  240.6 2.2 unpack.5
  242.8 2.2 unpack.6
  245.1 2.2 unpack.7
  247.3 2.6 %combine.1 = bf16[128,7168]{1,0:T(8,128)(2,1)} custom-call(bf16[192,128]{1,0:T(8,128)(2,1)S(1)} %get-tuple-element.34.table_ref, bf16[192,1792]{1,0:T(8,128)(2,1)S(1)} %bitcast.22), custom_call_target="tpu_custom_call" | custom-call | tf_op jit(solution)/shard_map/combine/pallas_call | solution.py:441
  (47 shorter events, 1.0 us)
Async XLA Ops:
  0.6 1.5 copy-start.4
  2.1 1.5 copy-start.5
  3.6 0.7 copy-start.15
  4.3 0.7 copy-start.16
  5.0 0.7 copy-start.17
  10.1 1.1 copy-start.13
  11.1 5.9 %copy-start = (bf16[1,7168,128]{2,1,0:T(8,128)(2,1)S(1)}, bf16[1,7168,128]{2,1,0:T(8,128)(2,1)}, u32[]{:S(2)}) copy-start(bf16[1,7168,128]{2,1,0:T(8,128)(2,1)} %param.13) | copy-start | bytes 5505028
  11.1 24.8 %all-to-all-start = ((bf16[8,48,1792]{2,1,0:T(8,128)(2,1)}), bf16[8,48,1792]{2,1,0:T(8,128)(2,1)S(1)}, u32[]{:S(2)}, u32[]{:S(2)}) async-start(bf16[8,48,1792]{2,1,0:T(8,128)(2,1)} %bitcast.24), calls=%async_computation | async-start | bytes 2752512 | tf_op jit(solution)/shard_map/all_to_all | solution.py:173
  17.1 1.5 copy-start.1
  20.7 33.6 %collective-permute-start.6 = (bf16[1792,384]{1,0:T(8,128)(2,1)}, bf16[1792,384]{1,0:T(8,128)(2,1)}, u32[]{:S(2)}, u32[]{:S(2)}) collective-permute-start(bf16[1792,384]{1,0:T(8,128)(2,1)} %pack_weights.5), channel_id=1, source_target_pairs={{0,4},{4,8},{8,12},{12,0},{16,20},{20,24},{24,28},{28,16},{32,36},... | collective-permute-start | bytes 4128776 | tf_op jit(solution)/shard_map/ppermute | solution.py:43
  38.0 9.6 %collective-permute-start = (bf16[48,3584]{1,0:T(8,128)(2,1)S(1)}, bf16[48,3584]{1,0:T(8,128)(2,1)S(1)}, u32[]{:S(2)}, u32[]{:S(2)}) collective-permute-start(bf16[48,3584]{1,0:T(8,128)(2,1)S(1)} %get-tuple-element.37), channel_id=1, source_target_pairs={{0,4},{4,8},{8,12},{12,0},{16,20},{20,24},{24,28},{28,16},{32,36},... | collective-permute-start | bytes 1032200 | tf_op jit(solution)/shard_map/ppermute | solution.py:43
  39.4 11.2 %collective-permute-start.1 = (bf16[48,3584]{1,0:T(8,128)(2,1)S(1)}, bf16[48,3584]{1,0:T(8,128)(2,1)S(1)}, u32[]{:S(2)}, u32[]{:S(2)}) collective-permute-start(bf16[48,3584]{1,0:T(8,128)(2,1)S(1)} %get-tuple-element.38), channel_id=1, source_target_pairs={{0,8},{4,12},{8,0},{12,4},{16,24},{20,28},{24,16},{28,20},{32,40},... | collective-permute-start | bytes 1032200 | tf_op jit(solution)/shard_map/ppermute | solution.py:43
  42.0 8.6 %collective-permute-start.2 = (bf16[48,3584]{1,0:T(8,128)(2,1)S(1)}, bf16[48,3584]{1,0:T(8,128)(2,1)S(1)}, u32[]{:S(2)}, u32[]{:S(2)}) collective-permute-start(bf16[48,3584]{1,0:T(8,128)(2,1)S(1)} %get-tuple-element.39), channel_id=1, source_target_pairs={{0,12},{4,0},{8,4},{12,8},{16,28},{20,16},{24,20},{28,24},{32,44},... | collective-permute-start | bytes 1032200 | tf_op jit(solution)/shard_map/ppermute | solution.py:43
  43.1 1.5 copy-start.2
  45.9 27.4 %collective-permute-start.7 = (bf16[1792,384]{1,0:T(8,128)(2,1)S(1)}, bf16[1792,384]{1,0:T(8,128)(2,1)}, u32[]{:S(2)}, u32[]{:S(2)}) collective-permute-start(bf16[1792,384]{1,0:T(8,128)(2,1)S(1)} %pack_weights.6), channel_id=1, source_target_pairs={{0,8},{4,12},{8,0},{12,4},{16,24},{20,28},{24,16},{28,20},{32,40},... | collective-permute-start | bytes 4128776 | tf_op jit(solution)/shard_map/ppermute | solution.py:43
  47.6 60.4 %collective-permute-start.8 = (bf16[1792,384]{1,0:T(8,128)(2,1)S(1)}, bf16[1792,384]{1,0:T(8,128)(2,1)}, u32[]{:S(2)}, u32[]{:S(2)}) collective-permute-start(bf16[1792,384]{1,0:T(8,128)(2,1)S(1)} %pack_weights.7), channel_id=1, source_target_pairs={{0,12},{4,0},{8,4},{12,8},{16,28},{20,16},{24,20},{28,24},{32,44},... | collective-permute-start | bytes 4128776 | tf_op jit(solution)/shard_map/ppermute | solution.py:43
  50.6 4.6 %copy-start.3 = (bf16[1,7168,128]{2,1,0:T(8,128)(2,1)S(1)}, bf16[1,7168,128]{2,1,0:T(8,128)(2,1)}, u32[]{:S(2)}) copy-start(bf16[1,7168,128]{2,1,0:T(8,128)(2,1)} %param.14) | copy-start | bytes 5505028
  50.7 57.3 %collective-permute-start.5 = (bf16[192,3584]{1,0:T(8,128)(2,1)S(1)}, bf16[192,3584]{1,0:T(8,128)(2,1)S(1)}, u32[]{:S(2)}, u32[]{:S(2)}) collective-permute-start(bf16[192,3584]{1,0:T(8,128)(2,1)S(1)} %line_up.1.refs_0_), channel_id=1, source_target_pairs={{0,32},{4,36},{8,40},{12,44},{16,48},{20,52},{24,56},{28,60},{32,0... | collective-permute-start | bytes 4128776 | tf_op jit(solution)/shard_map/ppermute | solution.py:43
  53.7 56.6 %collective-permute-start.4 = (bf16[192,3584]{1,0:T(8,128)(2,1)S(1)}, bf16[192,3584]{1,0:T(8,128)(2,1)S(1)}, u32[]{:S(2)}, u32[]{:S(2)}) collective-permute-start(bf16[192,3584]{1,0:T(8,128)(2,1)S(1)} %line_up.1.refs_0_), channel_id=1, source_target_pairs={{0,48},{4,52},{8,56},{12,60},{16,0},{20,4},{24,8},{28,12},{32,16},... | collective-permute-start | bytes 4128776 | tf_op jit(solution)/shard_map/ppermute | solution.py:43
  54.4 55.9 %collective-permute-start.3 = (bf16[192,3584]{1,0:T(8,128)(2,1)S(1)}, bf16[192,3584]{1,0:T(8,128)(2,1)S(1)}, u32[]{:S(2)}, u32[]{:S(2)}) collective-permute-start(bf16[192,3584]{1,0:T(8,128)(2,1)S(1)} %line_up.1.refs_0_), channel_id=1, source_target_pairs={{0,16},{4,20},{8,24},{12,28},{16,32},{20,36},{24,40},{28,44},{32,4... | collective-permute-start | bytes 4128776 | tf_op jit(solution)/shard_map/ppermute | solution.py:43
  56.5 1.1 copy-start.14
  108.0 2.3 copy-start.18
  110.3 1.1 copy-start.6
  111.4 71.2 %copy-start.8 = (bf16[192,3584]{1,0:T(8,128)(2,1)}, bf16[192,3584]{1,0:T(8,128)(2,1)S(1)}, u32[]{:S(2)}) copy-start(bf16[192,3584]{1,0:T(8,128)(2,1)S(1)} %collective-permute-done.3.refs_1_) | copy-start | bytes 4128772
  121.1 18.5 %collective-permute-start.9 = (bf16[768,384]{1,0:T(8,128)(2,1)S(1)}, bf16[768,384]{1,0:T(8,128)(2,1)S(1)}, u32[]{:S(2)}, u32[]{:S(2)}) collective-permute-start(bf16[768,384]{1,0:T(8,128)(2,1)S(1)} %get-tuple-element.41), channel_id=1, source_target_pairs={{0,12},{4,0},{8,4},{12,8},{16,28},{20,16},{24,20},{28,24},{32,44},... | collective-permute-start | bytes 1769480 | tf_op jit(solution)/shard_map/ppermute | solution.py:43
  126.5 13.2 %collective-permute-start.10 = (bf16[768,384]{1,0:T(8,128)(2,1)S(1)}, bf16[768,384]{1,0:T(8,128)(2,1)S(1)}, u32[]{:S(2)}, u32[]{:S(2)}) collective-permute-start(bf16[768,384]{1,0:T(8,128)(2,1)S(1)} %get-tuple-element.42), channel_id=1, source_target_pairs={{0,8},{4,12},{8,0},{12,4},{16,24},{20,28},{24,16},{28,20},{32,40},... | collective-permute-start | bytes 1769480 | tf_op jit(solution)/shard_map/ppermute | solution.py:43
  126.5 16.3 %collective-permute-start.11 = (bf16[768,384]{1,0:T(8,128)(2,1)S(1)}, bf16[768,384]{1,0:T(8,128)(2,1)S(1)}, u32[]{:S(2)}, u32[]{:S(2)}) collective-permute-start(bf16[768,384]{1,0:T(8,128)(2,1)S(1)} %get-tuple-element.43), channel_id=1, source_target_pairs={{0,4},{4,8},{8,12},{12,0},{16,20},{20,24},{24,28},{28,16},{32,36},... | collective-permute-start | bytes 1769480 | tf_op jit(solution)/shard_map/ppermute | solution.py:43
  143.3 25.2 %copy-start.11 = (bf16[768,384]{1,0:T(8,128)(2,1)}, bf16[768,384]{1,0:T(8,128)(2,1)S(1)}, u32[]{:S(2)}) copy-start(bf16[768,384]{1,0:T(8,128)(2,1)S(1)} %activate.1.refs_0_.refs_4_) | copy-start | bytes 1769476
  143.3 28.6 %copy-start.7 = (bf16[192,3584]{1,0:T(8,128)(2,1)S(1)}, bf16[192,3584]{1,0:T(8,128)(2,1)}, u32[]{:S(2)}) copy-start(bf16[192,3584]{1,0:T(8,128)(2,1)} %copy-done.6) | copy-start | bytes 4128772
  143.3 9.1 %collective-permute-start.14 = (bf16[768,384]{1,0:T(8,128)(2,1)S(1)}, bf16[768,384]{1,0:T(8,128)(2,1)S(1)}, u32[]{:S(2)}, u32[]{:S(2)}) collective-permute-start(bf16[768,384]{1,0:T(8,128)(2,1)S(1)} %activate.1.refs_0_.refs_4_), channel_id=1, source_target_pairs={{0,12},{4,0},{8,4},{12,8},{16,28},{20,16},{24,20},{28,24},{32,44},... | collective-permute-start | bytes 1769480 | tf_op jit(solution)/shard_map/ppermute | solution.py:43
  144.1 10.6 %collective-permute-start.13 = (bf16[768,384]{1,0:T(8,128)(2,1)S(1)}, bf16[768,384]{1,0:T(8,128)(2,1)S(1)}, u32[]{:S(2)}, u32[]{:S(2)}) collective-permute-start(bf16[768,384]{1,0:T(8,128)(2,1)S(1)} %activate.1.refs_0_.refs_4_), channel_id=1, source_target_pairs={{0,8},{4,12},{8,0},{12,4},{16,24},{20,28},{24,16},{28,20},{32,40},... | collective-permute-start | bytes 1769480 | tf_op jit(solution)/shard_map/ppermute | solution.py:43
  144.3 16.7 %collective-permute-start.12 = (bf16[768,384]{1,0:T(8,128)(2,1)S(1)}, bf16[768,384]{1,0:T(8,128)(2,1)S(1)}, u32[]{:S(2)}, u32[]{:S(2)}) collective-permute-start(bf16[768,384]{1,0:T(8,128)(2,1)S(1)} %activate.1.refs_0_.refs_4_), channel_id=1, source_target_pairs={{0,4},{4,8},{8,12},{12,0},{16,20},{20,24},{24,28},{28,16},{32,36},... | collective-permute-start | bytes 1769480 | tf_op jit(solution)/shard_map/ppermute | solution.py:43
  168.4 18.7 %collective-permute-start.15 = (bf16[192,1792]{1,0:T(8,128)(2,1)S(1)}, bf16[192,1792]{1,0:T(8,128)(2,1)S(1)}, u32[]{:S(2)}, u32[]{:S(2)}) collective-permute-start(bf16[192,1792]{1,0:T(8,128)(2,1)S(1)} %get-tuple-element.45), channel_id=1, source_target_pairs={{0,48},{4,52},{8,56},{12,60},{16,0},{20,4},{24,8},{28,12},{32,16},... | collective-permute-start | bytes 2064392 | tf_op jit(solution)/shard_map/ppermute | solution.py:43
  170.6 20.0 %collective-permute-start.16 = (bf16[192,1792]{1,0:T(8,128)(2,1)S(1)}, bf16[192,1792]{1,0:T(8,128)(2,1)S(1)}, u32[]{:S(2)}, u32[]{:S(2)}) collective-permute-start(bf16[192,1792]{1,0:T(8,128)(2,1)S(1)} %get-tuple-element.46), channel_id=1, source_target_pairs={{0,16},{4,20},{8,24},{12,28},{16,32},{20,36},{24,40},{28,44},{32,4... | collective-permute-start | bytes 2064392 | tf_op jit(solution)/shard_map/ppermute | solution.py:43
  170.6 20.0 %collective-permute-start.17 = (bf16[192,1792]{1,0:T(8,128)(2,1)S(1)}, bf16[192,1792]{1,0:T(8,128)(2,1)S(1)}, u32[]{:S(2)}, u32[]{:S(2)}) collective-permute-start(bf16[192,1792]{1,0:T(8,128)(2,1)S(1)} %get-tuple-element.47), channel_id=1, source_target_pairs={{0,32},{4,36},{8,40},{12,44},{16,48},{20,52},{24,56},{28,60},{32,0... | collective-permute-start | bytes 2064392 | tf_op jit(solution)/shard_map/ppermute | solution.py:43
  176.5 64.1 %collective-permute-start.23 = (bf16[1792,384]{1,0:T(8,128)(2,1)}, bf16[1792,384]{1,0:T(8,128)(2,1)}, u32[]{:S(2)}, u32[]{:S(2)}) collective-permute-start(bf16[1792,384]{1,0:T(8,128)(2,1)} %weight_grads.6), channel_id=1, source_target_pairs={{0,12},{4,0},{8,4},{12,8},{16,28},{20,16},{24,20},{28,24},{32,44},... | collective-permute-start | bytes 4128776 | tf_op jit(solution)/shard_map/ppermute | solution.py:43
  181.4 61.4 %collective-permute-start.22 = (bf16[1792,384]{1,0:T(8,128)(2,1)}, bf16[1792,384]{1,0:T(8,128)(2,1)}, u32[]{:S(2)}, u32[]{:S(2)}) collective-permute-start(bf16[1792,384]{1,0:T(8,128)(2,1)} %weight_grads.5), channel_id=1, source_target_pairs={{0,4},{4,8},{8,12},{12,0},{16,20},{20,24},{24,28},{28,16},{32,36},... | collective-permute-start | bytes 4128776 | tf_op jit(solution)/shard_map/ppermute | solution.py:43
  187.1 58.0 %collective-permute-start.21 = (bf16[1792,384]{1,0:T(8,128)(2,1)}, bf16[1792,384]{1,0:T(8,128)(2,1)}, u32[]{:S(2)}, u32[]{:S(2)}) collective-permute-start(bf16[1792,384]{1,0:T(8,128)(2,1)} %weight_grads.4), channel_id=1, source_target_pairs={{0,8},{4,12},{8,0},{12,4},{16,24},{20,28},{24,16},{28,20},{32,40},... | collective-permute-start | bytes 4128776 | tf_op jit(solution)/shard_map/ppermute | solution.py:43
  191.0 32.2 %collective-permute-start.18 = (bf16[48,1792]{1,0:T(8,128)(2,1)S(1)}, bf16[48,1792]{1,0:T(8,128)(2,1)S(1)}, u32[]{:S(2)}, u32[]{:S(2)}) collective-permute-start(bf16[48,1792]{1,0:T(8,128)(2,1)S(1)} %get-tuple-element.49), channel_id=1, source_target_pairs={{0,4},{4,8},{8,12},{12,0},{16,20},{20,24},{24,28},{28,16},{32,36},... | collective-permute-start | bytes 516104 | tf_op jit(solution)/shard_map/ppermute | solution.py:43
  191.1 32.1 %collective-permute-start.19 = (bf16[48,1792]{1,0:T(8,128)(2,1)S(1)}, bf16[48,1792]{1,0:T(8,128)(2,1)S(1)}, u32[]{:S(2)}, u32[]{:S(2)}) collective-permute-start(bf16[48,1792]{1,0:T(8,128)(2,1)S(1)} %get-tuple-element.50), channel_id=1, source_target_pairs={{0,8},{4,12},{8,0},{12,4},{16,24},{20,28},{24,16},{28,20},{32,40},... | collective-permute-start | bytes 516104 | tf_op jit(solution)/shard_map/ppermute | solution.py:43
  223.1 4.6 %collective-permute-start.20 = (bf16[48,1792]{1,0:T(8,128)(2,1)S(1)}, bf16[48,1792]{1,0:T(8,128)(2,1)S(1)}, u32[]{:S(2)}, u32[]{:S(2)}) collective-permute-start(bf16[48,1792]{1,0:T(8,128)(2,1)S(1)} %get-tuple-element.51), channel_id=1, source_target_pairs={{0,12},{4,0},{8,4},{12,8},{16,28},{20,16},{24,20},{28,24},{32,44},... | collective-permute-start | bytes 516104 | tf_op jit(solution)/shard_map/ppermute | solution.py:43
  228.6 0.9 copy-start.10
  229.4 17.9 %all-to-all-start.1 = ((bf16[8,24,1792]{2,1,0:T(8,128)(2,1)}), bf16[8,24,1792]{2,1,0:T(8,128)(2,1)S(1)}, u32[]{:S(2)}, u32[]{:S(2)}) async-start(bf16[8,24,1792]{2,1,0:T(8,128)(2,1)} %bitcast.23), calls=%async_computation.1 | async-start | bytes 1376256 | tf_op jit(solution)/shard_map/all_to_all | solution.py:173
  233.5 1.3 copy-start.9
  234.8 1.1 copy-start.12
